TPU v7x, 32 devices: a whole 2x2x4 slice. The times are simulated.
32 devices in a mesh: wide: 16 (over z, y, x), narrow: 2 (over core).
Axes of the slice: x: 2, y: 2, z: 4, core: 2. Of those that a mesh axis runs over, the one named last changes fastest.
Arguments:
- tokens: bfloat16 [8192, 1024], P(('wide', 'narrow')), may hold values from -6 to 6
- seq_lens: int32 [16, 1], P('wide'), may hold values from 1 to 512, as said below
- decay_rate: float32 [8], replicated, may hold values from 0.0001 to 0.03
- w_query: bfloat16 [1024, 1024], replicated, may hold values from -0.1875 to 0.1875
- w_key: bfloat16 [1024, 1024], replicated, may hold values from -0.1875 to 0.1875
- w_value: bfloat16 [1024, 1024], replicated, may hold values from -0.1875 to 0.1875
- w_gate_u: bfloat16 [1024, 1024], replicated, may hold values from -0.1875 to 0.1875
- w_out: bfloat16 [1024, 1024], replicated, may hold values from -0.1875 to 0.1875
- w_left: bfloat16 [1024, 2816], P(None, 'narrow'), may hold values from -0.1875 to 0.1875
- w_right: bfloat16 [1024, 2816], P(None, 'narrow'), may hold values from -0.1875 to 0.1875
- w_down: bfloat16 [2816, 1024], P('narrow'), may hold values from -0.109375 to 0.109375
- cotangent: bfloat16 [8192, 1024], P(('wide', 'narrow')), may hold values from -6 to 6
Outputs:
- mixed: bfloat16 [8192, 1024], P(('wide', 'narrow'))
- input_grad: float32 [8192, 1024], P(('wide', 'narrow'))
- grad_query: float32 [1024, 1024], P('wide')
- grad_key: float32 [1024, 1024], P('wide')
- grad_value: float32 [1024, 1024], P('wide')
- grad_gate_u: float32 [1024, 1024], P('wide')
- grad_out: float32 [1024, 1024], P('wide')
- grad_left: float32 [1024, 2816], P('wide', 'narrow')
- grad_right: float32 [1024, 2816], P('wide', 'narrow')
- grad_down: float32 [2816, 1024], P('narrow', 'wide')
Inputs may be any that keep to these rules, and one draw needn't show every extreme that they name: `seq_lens`: row g holds the lengths of the 1 sequence of group g; padded to whole blocks of 256 rows they add up to at most 512.
All inputs are finite; a program needn't handle non-finite values.
Results may differ from a plain program's by a relative error of at most 0.013.
Values may be sent and summed in bfloat16 or wider, within the bound.
No kernel may reach another device: no remote copies, remote signals or barrier semaphores. Data moves between devices by JAX's collectives and lax.ppermute only.
A program may use at most 192 MiB of HBM per device.

v0:
```python
import jax
import jax.numpy as jnp
from jax import lax
from jax.sharding import PartitionSpec as P

BLOCK = 256


EPSILON = 1e-06


def shifted(block, axis, distance):
    devices = range(lax.axis_size(axis))
    route = [(i - distance, i) for i in devices if i - distance in devices]
    return lax.ppermute(block, axis, route)


def rms_scaled(values):
    return values * lax.rsqrt(jnp.mean(values * values, axis=-1, keepdims=True) + EPSILON)


def rms_back(values, upstream):
    scale = lax.rsqrt(jnp.mean(values * values, axis=-1, keepdims=True) + EPSILON)
    normed = values * scale
    return scale * (upstream - normed * jnp.mean(upstream * normed, axis=-1, keepdims=True))


def silu_slope(values):
    sigmoid = jax.nn.sigmoid(values)
    return sigmoid * (1.0 + values * (1.0 - sigmoid))


def dot_plain(left_side, right_side):
    return jnp.dot(left_side, right_side, preferred_element_type=jnp.float32)


def dot_against(left_side, right_side):
    return lax.dot_general(
        left_side, right_side, (((1,), (1,)), ((), ())), preferred_element_type=jnp.float32
    )


def dot_outer(left_side, right_side):
    return lax.dot_general(
        left_side, right_side, (((0,), (0,)), ((), ())), preferred_element_type=jnp.float32
    )


def exact_sum(form, left_side, right_side):
    return jnp.einsum(form, left_side, right_side, precision=lax.Precision.HIGHEST)


def layout(lengths, first_row, row_count, block_rows):
    padded = (lengths + block_rows - 1) // block_rows * block_rows
    ends = jnp.cumsum(padded)
    starts = ends - padded
    positions = first_row + jnp.arange(row_count, dtype=jnp.int32)
    sequence = jnp.sum((positions[:, None] >= ends[None, :]).astype(jnp.int32), axis=1)
    slots = jnp.arange(lengths.shape[0], dtype=jnp.int32)
    member = (sequence[:, None] == slots[None, :]).astype(jnp.int32)
    row_start = jnp.sum(member * starts[None, :], axis=1)
    row_length = jnp.sum(member * lengths[None, :], axis=1)
    offset = positions - row_start
    inside = sequence < lengths.shape[0]
    usable = jnp.logical_and(inside, offset < row_length)
    fresh = jnp.logical_not(jnp.logical_and(inside, offset > 0))
    return (usable, fresh, sequence)


def on_device(
    tokens,
    seq_lens,
    decay_rate,
    w_query,
    w_key,
    w_value,
    w_gate_u,
    w_out,
    w_left,
    w_right,
    w_down,
    cotangent,
):
    row_count, model_width = tokens.shape
    head_count = decay_rate.shape[0]
    head_size = model_width // head_count
    block_count = row_count // BLOCK
    block_shape = (block_count, BLOCK, head_count, head_size)
    narrow_index = lax.axis_index("narrow")
    usable, fresh, sequence = layout(seq_lens[0], narrow_index * row_count, row_count + 1, BLOCK)
    valid = usable[:row_count].astype(jnp.float32)[:, None]
    fresh_blocks = fresh[:row_count].reshape(block_count, BLOCK)[:, 0]
    carry_in = jnp.logical_not(fresh[0]).astype(jnp.float32)
    carry_out = jnp.logical_not(fresh[row_count]).astype(jnp.float32)
    steps = jnp.arange(BLOCK, dtype=jnp.float32)
    spacing = steps[:, None] - steps[None, :]
    decay_mask = jnp.where(
        spacing[None] >= 0,
        jnp.exp(-decay_rate[:, None, None] * jnp.maximum(spacing, 0.0)[None]),
        0.0,
    )
    query_decay = jnp.exp(-decay_rate[None, :] * (steps[:, None] + 1.0))
    key_decay = jnp.exp(-decay_rate[None, :] * (BLOCK - 1.0 - steps[:, None]))
    carry_rate = jnp.exp(-decay_rate * BLOCK)
    inputs = tokens.astype(jnp.float32)
    normed_in = rms_scaled(inputs).astype(jnp.bfloat16)
    query_pre = dot_plain(normed_in, w_query)
    key_pre = dot_plain(normed_in, w_key)
    value_pre = dot_plain(normed_in, w_value)
    gate_pre = dot_plain(normed_in, w_gate_u)
    queries = jax.nn.silu(query_pre).astype(jnp.bfloat16)
    keys = (jax.nn.silu(key_pre) * valid).astype(jnp.bfloat16)
    values = (value_pre * valid).astype(jnp.bfloat16)
    gate_u = jax.nn.silu(gate_pre)
    query_blocks = queries.reshape(block_shape)
    key_blocks = keys.reshape(block_shape)
    value_blocks = values.reshape(block_shape)
    scores = jnp.einsum(
        "nihe,njhe->nhij", query_blocks, key_blocks, preferred_element_type=jnp.float32
    )
    weighted = (scores * decay_mask[None]).astype(jnp.bfloat16)
    within = jnp.einsum(
        "nhij,njhe->nihe", weighted, value_blocks, preferred_element_type=jnp.float32
    )
    query_wide = query_blocks.astype(jnp.float32) * query_decay[None, :, :, None]
    key_wide = key_blocks.astype(jnp.float32) * key_decay[None, :, :, None]
    value_wide = value_blocks.astype(jnp.float32)
    block_states = exact_sum("njhe,njhf->nhef", key_wide, value_wide)

    def advance(state, item):
        block_state, reset = item
        prior = jnp.where(reset, 0.0, state)
        return (carry_rate[:, None, None] * prior + block_state, prior)

    state_local, _ = lax.scan(
        advance, jnp.zeros_like(block_states[0]), (block_states, fresh_blocks)
    )
    state_in = shifted(state_local, "narrow", 1) * carry_in
    _, priors = lax.scan(advance, state_in, (block_states, fresh_blocks))
    across = exact_sum("nihe,nhef->nihf", query_wide, priors)
    attended = (within + across).reshape(row_count, model_width)
    attn_normed = rms_scaled(attended)
    gated = (attn_normed * gate_u).astype(jnp.bfloat16)
    branch = dot_plain(gated, w_out)
    hidden_res = inputs + valid * branch
    normed_mid = rms_scaled(hidden_res).astype(jnp.bfloat16)
    mid_rows = lax.all_gather(normed_mid, "narrow", axis=0, tiled=True)
    left_part = dot_plain(mid_rows, w_left)
    right_part = dot_plain(mid_rows, w_right)
    joined = (left_part * right_part).astype(jnp.bfloat16)
    ffn_out = lax.psum_scatter(dot_plain(joined, w_down), "narrow", scatter_dimension=0, tiled=True)
    mixed = (hidden_res + valid * ffn_out).astype(jnp.bfloat16)
    upstream = cotangent.astype(jnp.float32)
    d_ffn = (valid * upstream).astype(jnp.bfloat16)
    d_ffn_rows = lax.all_gather(d_ffn, "narrow", axis=0, tiled=True)
    grad_down_part = dot_outer(joined, d_ffn_rows)
    d_joined = dot_against(d_ffn_rows, w_down)
    d_left = (d_joined * right_part).astype(jnp.bfloat16)
    d_right = (d_joined * left_part).astype(jnp.bfloat16)
    grad_left = dot_outer(mid_rows, d_left)
    grad_right = dot_outer(mid_rows, d_right)
    d_mid = lax.psum_scatter(
        dot_against(d_left, w_left) + dot_against(d_right, w_right),
        "narrow",
        scatter_dimension=0,
        tiled=True,
    )
    d_hidden = upstream + rms_back(hidden_res, d_mid)
    d_branch = (valid * d_hidden).astype(jnp.bfloat16)
    grad_out = dot_outer(gated, d_branch)
    d_gated = dot_against(d_branch, w_out)
    d_gate_pre = (d_gated * attn_normed * silu_slope(gate_pre)).astype(jnp.bfloat16)
    d_attended = rms_back(attended, d_gated * gate_u).astype(jnp.bfloat16)
    grad_blocks = d_attended.reshape(block_shape)
    d_weighted = jnp.einsum(
        "nihe,njhe->nhij", grad_blocks, value_blocks, preferred_element_type=jnp.float32
    )
    d_scores = (d_weighted * decay_mask[None]).astype(jnp.bfloat16)
    d_query_blocks = jnp.einsum(
        "nhij,njhe->nihe", d_scores, key_blocks, preferred_element_type=jnp.float32
    )
    d_key_blocks = jnp.einsum(
        "nhij,nihe->njhe", d_scores, query_blocks, preferred_element_type=jnp.float32
    )
    d_value_blocks = jnp.einsum(
        "nhij,nihe->njhe", weighted, grad_blocks, preferred_element_type=jnp.float32
    )
    grad_wide = grad_blocks.astype(jnp.float32)
    d_query_blocks = (
        d_query_blocks
        + exact_sum("nihf,nhef->nihe", grad_wide, priors) * query_decay[None, :, :, None]
    )
    prior_grads = exact_sum("nihe,nihf->nhef", query_wide, grad_wide)

    def retreat(after, item):
        prior_grad, reset = item
        through = prior_grad + carry_rate[:, None, None] * after
        return (jnp.where(reset, 0.0, through), after)

    state_in_grad, _ = lax.scan(
        retreat, jnp.zeros_like(prior_grads[0]), (prior_grads, fresh_blocks), reverse=True
    )
    state_out_grad = (
        shifted(state_in_grad.astype(jnp.bfloat16), "narrow", -1).astype(state_in_grad.dtype)
        * carry_out
    )
    _, state_grads = lax.scan(retreat, state_out_grad, (prior_grads, fresh_blocks), reverse=True)
    d_key_blocks = (
        d_key_blocks
        + exact_sum("njhf,nhef->njhe", value_wide, state_grads) * key_decay[None, :, :, None]
    )
    d_value_blocks = d_value_blocks + exact_sum("njhe,nhef->njhf", key_wide, state_grads)
    d_queries = d_query_blocks.reshape(row_count, model_width)
    d_keys = d_key_blocks.reshape(row_count, model_width)
    d_values = d_value_blocks.reshape(row_count, model_width)
    d_query_pre = (d_queries * silu_slope(query_pre)).astype(jnp.bfloat16)
    d_key_pre = (d_keys * valid * silu_slope(key_pre)).astype(jnp.bfloat16)
    d_value_pre = (d_values * valid).astype(jnp.bfloat16)
    grad_query = dot_outer(normed_in, d_query_pre)
    grad_key = dot_outer(normed_in, d_key_pre)
    grad_value = dot_outer(normed_in, d_value_pre)
    grad_gate_u = dot_outer(normed_in, d_gate_pre)
    d_in = (
        dot_against(d_query_pre, w_query)
        + dot_against(d_key_pre, w_key)
        + dot_against(d_value_pre, w_value)
        + dot_against(d_gate_pre, w_gate_u)
    )
    input_grad = d_hidden + rms_back(inputs, d_in)
    grad_query, grad_key, grad_value, grad_gate_u, grad_out = lax.psum(
        (grad_query, grad_key, grad_value, grad_gate_u, grad_out), "narrow"
    )
    summed = (
        lax.psum_scatter(grad_query, "wide", scatter_dimension=0, tiled=True),
        lax.psum_scatter(grad_key, "wide", scatter_dimension=0, tiled=True),
        lax.psum_scatter(grad_value, "wide", scatter_dimension=0, tiled=True),
        lax.psum_scatter(grad_gate_u, "wide", scatter_dimension=0, tiled=True),
        lax.psum_scatter(grad_out, "wide", scatter_dimension=0, tiled=True),
        lax.psum_scatter(grad_left, "wide", scatter_dimension=0, tiled=True),
        lax.psum_scatter(grad_right, "wide", scatter_dimension=0, tiled=True),
    )
    grad_down = lax.psum_scatter(grad_down_part, "wide", scatter_dimension=1, tiled=True)
    grad_query, grad_key, grad_value, grad_gate_u, grad_out = (
        summed[0],
        summed[1],
        summed[2],
        summed[3],
        summed[4],
    )
    return (
        mixed,
        input_grad,
        grad_query,
        grad_key,
        grad_value,
        grad_gate_u,
        grad_out,
        summed[5],
        summed[6],
        grad_down,
    )


def solution(mesh):
    placed = (
        P(("wide", "narrow"), None),
        P("wide", None),
        P(),
        P(),
        P(),
        P(),
        P(),
        P(),
        P(None, "narrow"),
        P(None, "narrow"),
        P("narrow", None),
        P(("wide", "narrow"), None),
    )
    return jax.shard_map(
        on_device,
        mesh=mesh,
        in_specs=placed,
        out_specs=(
            P(("wide", "narrow"), None),
            P(("wide", "narrow"), None),
            P("wide", None),
            P("wide", None),
            P("wide", None),
            P("wide", None),
            P("wide", None),
            P("wide", "narrow"),
            P("wide", "narrow"),
            P("narrow", "wide"),
        ),
        check_vma=False,
    )
```

profile of v0, /device:TPU:0, one launch (start us, length us, event | category | flops | bytes accessed | tf_op | source)
XLA Modules:
  0.0 1019.6 jit_solution(6646679989402866855)
XLA Ops:
  8.1 1.4 fusion.16
  10.2 2.5 fusion.71
  14.2 1.2 fusion.11
  15.4 2.2 convolution_add_fusion.7
  17.6 3.2 collective-permute-start
  23.3 2.0 multiply_convert_fusion.13
  25.2 2.0 copy.52
  27.3 2.0 multiply_convert_fusion.4
  30.8 3.8 fusion.17
  34.6 2.6 copy.48
  37.2 3.9 multiply_convert_fusion.11
  44.9 10.3 %all-gather.3.cloned.1.call-done = bf16[512,1024]{1,0:T(8,128)(2,1)} async-done(((bf16[256,1024]{1,0:T(8,128)(2,1)}), bf16[512,1024]{1,0:T(8,128)(2,1)}) %all-gather.3.cloned.1.call-update) | async-done | bytes 1048592 | tf_op jit(solution)/shard_map/all_gather | solution.py:147
  55.2 5.7 fusion.78
  60.8 3.4 fusion.77
  64.2 2.8 all-gather.5.cloned.1.call-done
  67.0 6.1 multiply_convert_fusion
  73.1 1.8 fusion.80
  75.9 3.2 convolution_add_fusion
  79.2 4.5 fusion.79
  83.8 6.3 reduce-scatter.13.cloned.1.call-done
  90.1 1.5 multiply_reduce_fusion.1
  91.6 11.5 %reduce-scatter.11.cloned.1.call-done = f32[256,1024]{1,0:T(8,128)} async-done(((f32[512,1024]{1,0:T(8,128)}), f32[256,1024]{1,0:T(8,128)}) %reduce-scatter.11.cloned.1.call-update) | async-done | bytes 1048592 | tf_op jit(solution)/shard_map/reduce_scatter | solution.py:151
  103.1 2.8 convert_add_fusion.1
  105.9 2.8 fusion.59
  108.7 1.1 copy-done.24
  109.9 2.9 multiply_reduce_fusion
  112.8 1.4 multiply_convert_fusion.5
  114.3 2.9 fusion.62
  119.9 3.3 fusion.4
  123.2 1.6 copy.49
  124.8 1.6 multiply_convert_fusion.8
  126.4 2.9 fusion.67
  130.4 1.4 fusion.10
  131.8 1.3 collective-permute-start.1
  133.7 1.5 convolution_bitcast_fusion.2
  135.3 1.6 fusion.6
  136.9 2.6 copy.50
  139.5 4.2 fusion.65
  143.8 1.5 fusion.82
  145.4 2.3 convolution_add_fusion.1
  147.7 1.6 copy.51
  149.3 2.9 fusion.61
  152.2 1.3 copy-done.37
  153.5 5.6 fusion.85
  159.4 1.0 copy-done.10
  160.5 5.5 fusion.84
  166.1 1.3 copy-done.8
  167.4 5.5 fusion.83
  174.0 3.3 fusion.81
  177.3 27.9 %reduce-scatter.29.cloned.1.call-done = f32[64,1024]{1,0:T(8,128)} async-done(((f32[1024,1024]{1,0:T(8,128)}), f32[64,1024]{1,0:T(8,128)}) %reduce-scatter.29.cloned.1.call-update) | async-done | bytes 262160 | tf_op jit(solution)/shard_map/reduce_scatter | solution.py:238
  205.2 96.9 %reduce-scatter.27.cloned.1.call-done = f32[64,1024]{1,0:T(8,128)} async-done(((f32[1024,1024]{1,0:T(8,128)}), f32[64,1024]{1,0:T(8,128)}) %reduce-scatter.27.cloned.1.call-update) | async-done | bytes 262160 | tf_op jit(solution)/shard_map/reduce_scatter | solution.py:237
  302.1 97.0 %reduce-scatter.21.cloned.1.call-done = f32[64,1024]{1,0:T(8,128)} async-done(((f32[1024,1024]{1,0:T(8,128)}), f32[64,1024]{1,0:T(8,128)}) %reduce-scatter.21.cloned.1.call-update) | async-done | bytes 262160 | tf_op jit(solution)/shard_map/reduce_scatter | solution.py:234
  399.1 97.0 %reduce-scatter.23.cloned.1.call-done = f32[64,1024]{1,0:T(8,128)} async-done(((f32[1024,1024]{1,0:T(8,128)}), f32[64,1024]{1,0:T(8,128)}) %reduce-scatter.23.cloned.1.call-update) | async-done | bytes 262160 | tf_op jit(solution)/shard_map/reduce_scatter | solution.py:235
  496.2 97.1 %reduce-scatter.25.cloned.1.call-done = f32[64,1024]{1,0:T(8,128)} async-done(((f32[1024,1024]{1,0:T(8,128)}), f32[64,1024]{1,0:T(8,128)}) %reduce-scatter.25.cloned.1.call-update) | async-done | bytes 262160 | tf_op jit(solution)/shard_map/reduce_scatter | solution.py:236
  593.3 3.2 convolution_add_fusion.5
  599.5 1.2 fusion.15
  600.7 120.8 %reduce-scatter.19.cloned.1.call-done = f32[1408,64]{0,1:T(8,128)} async-done(((f32[1408,1024]{0,1:T(8,128)}), f32[1408,64]{0,1:T(8,128)}) %reduce-scatter.19.cloned.1.call-update) | async-done | bytes 360464 | tf_op jit(solution)/shard_map/reduce_scatter | solution.py:242
  721.5 129.9 %reduce-scatter.17.cloned.1.call-done = f32[64,1408]{1,0:T(8,128)} async-done(((f32[1024,1408]{1,0:T(8,128)}), f32[64,1408]{1,0:T(8,128)}) %reduce-scatter.17.cloned.1.call-update) | async-done | bytes 360464 | tf_op jit(solution)/shard_map/reduce_scatter | solution.py:240
  851.5 129.8 %reduce-scatter.15.cloned.1.call-done = f32[64,1408]{1,0:T(8,128)} async-done(((f32[1024,1408]{1,0:T(8,128)}), f32[64,1408]{1,0:T(8,128)}) %reduce-scatter.15.cloned.1.call-update) | async-done | bytes 360464 | tf_op jit(solution)/shard_map/reduce_scatter | solution.py:239
  981.2 24.0 %all-reduce.3.cloned.1.call-done = (f32[64,1024]{1,0:T(8,128)}, f32[64,1024]{1,0:T(8,128)}, f32[64,1024]{1,0:T(8,128)}, f32[64,1024]{1,0:T(8,128)}, f32[64,1024]{1,0:T(8,128)}) async-done(((f32[64,1024]{1,0:T(8,128)}, f32[64,1024]{1,0:T(8,128)}, f32[64,1024]{1,0:T(8,128)}, f32[64,1024]{1,0:T(8,128)}, f32[64,1024]{1,0:T(8,128)}), (f32[64,1024]{1,0:T(8,128)}, f32[64,1024]{1,0:T(8,128)}, f32[64,1024]{1,0:T(8,128)}, ...) | async-done | bytes 1310736 | tf_op jit(solution)/shard_map/psum | solution.py:230
  1005.2 1.7 copy.94
  1006.9 1.7 copy.95
  1008.6 1.7 copy.96
  1010.2 1.7 copy.97
  (144 shorter events, 19.5 us)
Async XLA Ops:
  7.2 59.8 %copy-start = (bf16[1408,1024]{1,0:T(8,128)(2,1)S(1)}, bf16[1408,1024]{1,0:T(8,128)(2,1)}, u32[]{:S(2)}) copy-start(bf16[1408,1024]{1,0:T(8,128)(2,1)} %param.22) | copy-start | bytes 8650756
  7.2 48.0 %all-gather.3.cloned.1.call-start = ((), (), s32[]{:S(2)}) async-start(), calls=%async_computation.10 | async-start | bytes 1572864 | tf_op jit(solution)/shard_map/all_gather | solution.py:147
  8.1 4.6 copy-start.2
  8.1 4.6 copy-start.32
  12.7 2.6 copy-start.19
  12.8 1.4 copy-start.34
  14.2 3.4 copy-start.27
  14.2 9.1 copy-start.31
  15.3 9.9 copy-start.11
  17.6 12.2 %collective-permute-start = (f32[8,128,128]{2,1,0:T(8,128)}, f32[8,128,128]{2,1,0:T(8,128)}, u32[]{:S(2)}, u32[]{:S(2)}) collective-permute-start(f32[8,128,128]{2,1,0:T(8,128)} %convolution_add_fusion.7), channel_id=1, source_target_pairs={{0,1},{2,3},{4,5},{6,7},{8,9},{10,11},{12,13},{14,15},{16,17},{18,... | collective-permute-start | bytes 1572872 | tf_op jit(solution)/shard_map/ppermute | solution.py:15
  27.3 2.0 copy-start.28
  29.3 5.3 copy-start.22
  29.3 1.4 copy-start.15
  37.2 3.9 copy-start.46
  41.1 0.9 copy-start.39
  42.0 1.0 copy-start.5
  43.9 23.0 %all-gather.5.cloned.1.call-start = ((), (), s32[]{:S(2)}) async-start(), calls=%async_computation.12 | async-start | bytes 1572864 | tf_op jit(solution)/shard_map/all_gather | solution.py:155
  44.7 45.4 %reduce-scatter.13.cloned.1.call-start = ((), (), s32[]{:S(2)}) async-start(), calls=%async_computation.13 | async-start | bytes 3145728 | tf_op jit(solution)/shard_map/reduce_scatter | solution.py:162
  55.2 5.7 copy-start.25
  55.2 5.7 copy-start.43
  67.0 6.1 copy-start.44
  73.1 1.8 copy-start.7
  73.1 1.8 copy-start.9
  73.1 2.9 copy-start.45
  79.2 23.9 %reduce-scatter.11.cloned.1.call-start = ((), (), s32[]{:S(2)}) async-start(), calls=%async_computation.11 | async-start | bytes 3145728 | tf_op jit(solution)/shard_map/reduce_scatter | solution.py:151
  83.7 6.4 copy-start.6
  83.7 19.4 %copy-start.35 = (bf16[256,1024]{1,0:T(8,128)(2,1)S(1)}, bf16[256,1024]{1,0:T(8,128)(2,1)}, u32[]{:S(2)}) copy-start(bf16[256,1024]{1,0:T(8,128)(2,1)} %param.23) | copy-start | bytes 1572868
  83.8 121.4 %reduce-scatter.29.cloned.1.call-start = ((), (), s32[]{:S(2)}) async-start(), calls=%async_computation.21 | async-start | bytes 4456448 | tf_op jit(solution)/shard_map/reduce_scatter | solution.py:238
  103.1 2.8 copy-start.40
  105.9 2.9 copy-start.3
  108.7 1.2 copy-start.24
  108.7 193.4 %reduce-scatter.27.cloned.1.call-start = ((), (), s32[]{:S(2)}) async-start(), calls=%async_computation.20 | async-start | bytes 4456448 | tf_op jit(solution)/shard_map/reduce_scatter | solution.py:237
  109.9 2.9 copy-start.38
  114.3 2.9 copy-start.17
  117.1 1.0 copy-start.36
  117.1 1.3 copy-start.29
  117.1 1.3 copy-start.41
  117.1 282.0 %reduce-scatter.21.cloned.1.call-start = ((), (), s32[]{:S(2)}) async-start(), calls=%async_computation.17 | async-start | bytes 4456448 | tf_op jit(solution)/shard_map/reduce_scatter | solution.py:234
  118.4 1.0 copy-start.12
  119.4 3.8 copy-start.23
  126.4 2.9 copy-start.13
  129.4 1.0 copy-start.16
  129.4 366.8 %reduce-scatter.23.cloned.1.call-start = ((), (), s32[]{:S(2)}) async-start(), calls=%async_computation.18 | async-start | bytes 4456448 | tf_op jit(solution)/shard_map/reduce_scatter | solution.py:235
  130.4 4.9 copy-start.30
  131.8 3.5 collective-permute-start.1
  136.9 2.6 copy-start.20
  143.8 449.5 %reduce-scatter.25.cloned.1.call-start = ((), (), s32[]{:S(2)}) async-start(), calls=%async_computation.19 | async-start | bytes 4456448 | tf_op jit(solution)/shard_map/reduce_scatter | solution.py:236
  152.1 1.4 copy-start.37
  152.2 569.4 %reduce-scatter.19.cloned.1.call-start = ((), (), s32[]{:S(2)}) async-start(), calls=%async_computation.16 | async-start | bytes 6127616 | tf_op jit(solution)/shard_map/reduce_scatter | solution.py:242
  159.1 1.4 copy-start.10
  159.1 692.3 %reduce-scatter.17.cloned.1.call-start = ((), (), s32[]{:S(2)}) async-start(), calls=%async_computation.15 | async-start | bytes 6127616 | tf_op jit(solution)/shard_map/reduce_scatter | solution.py:240
  166.0 1.4 copy-start.8
  166.0 815.2 %reduce-scatter.15.cloned.1.call-start = ((), (), s32[]{:S(2)}) async-start(), calls=%async_computation.14 | async-start | bytes 6127616 | tf_op jit(solution)/shard_map/reduce_scatter | solution.py:239
  172.9 1.0 copy-start.14
  172.9 420.3 %copy-start.21 = (f32[256,1024]{1,0:T(8,128)S(1)}, f32[256,1024]{1,0:T(8,128)}, u32[]{:S(2)}) copy-start(f32[256,1024]{1,0:T(8,128)} %copy-done.19) | copy-start | bytes 3145732
  172.9 832.2 %all-reduce.3.cloned.1.call-start = ((), (), s32[]{:S(2)}) async-start(), calls=%async_computation.22 | async-start | bytes 2621440 | tf_op jit(solution)/shard_map/psum | solution.py:230
  593.3 3.2 copy-start.33
  596.5 1.0 copy-start.18
  596.5 1.8 copy-start.26
  598.3 1.2 copy-start.4
  599.5 413.1 %copy-start.1 = (bf16[1408,1024]{1,0:T(8,128)(2,1)S(1)}, bf16[1408,1024]{1,0:T(8,128)(2,1)}, u32[]{:S(2)}) copy-start(bf16[1408,1024]{1,0:T(8,128)(2,1)} %param.22) | copy-start | bytes 8650756
  1005.2 6.7 copy-start.42
Sparse Core Ops, SparseCore 0:
  44.0 11.1 all-gather.2
  56.7 10.1 all-gather.4
  79.3 10.7 reduce-scatter.12
  92.3 10.7 reduce-scatter.10
  108.8 96.3 reduce-scatter.28
  207.3 94.7 reduce-scatter.26
  304.4 94.7 reduce-scatter.20
  401.4 94.7 reduce-scatter.22
  498.5 94.7 reduce-scatter.24
  596.0 125.5 reduce-scatter.18
  724.4 126.9 reduce-scatter.16
  854.2 126.9 reduce-scatter.14
  983.9 21.2 all-reduce.2
where the time goes:
time: 1030 us; the launch traced here: 1020 us
  waiting for transfers between devices  852 us (83%)
  matrix products  99.4 us (10%)
  local copies, waits for them, and re-layouts  31.8 us (3%)
  between operations  16.9 us (2%)
  other arithmetic  13.6 us (1%)
    reduce_scatter x1, waiting for transfers between devices, on_device(): lax.psum_scatter(grad_right, 'wide', scatter_dimension=0, tiled=True)  130 us
    reduce_scatter x1, waiting for transfers between devices, on_device(): lax.psum_scatter(grad_left, 'wide', scatter_dimension=0, tiled=True)  130 us
    reduce_scatter x1, waiting for transfers between devices, on_device(): lax.psum_scatter(grad_down_part, 'wide', scatter_dimension=1, tiled=True)  121 us
    reduce_scatter x1, waiting for transfers between devices, on_device(): lax.psum_scatter(grad_value, 'wide', scatter_dimension=0, tiled=True)  97.1 us
    reduce_scatter x1, waiting for transfers between devices, on_device(): lax.psum_scatter(grad_query, 'wide', scatter_dimension=0, tiled=True)  97 us
    reduce_scatter x1, waiting for transfers between devices, on_device(): lax.psum_scatter(grad_key, 'wide', scatter_dimension=0, tiled=True)  97 us
    reduce_scatter x1, waiting for transfers between devices, on_device(): lax.psum_scatter(grad_gate_u, 'wide', scatter_dimension=0, tiled=True)  96.9 us
    dot_general x8, matrix products, dot_outer(): lax.dot_general(left_side, right_side, (((0,), (0,)), ((), ())), preferre...  32.3 us
  transfers between devices with their start and end apart: 15, of which 13 were waited for; matrix products, arithmetic and copies ran while one was open for 9% of the time, Pallas kernels for 0%

commit v1 on v0

v1 whole, which is shorter than its diff:
```python
import functools

import jax
import jax.numpy as jnp
from jax import lax
from jax.experimental import pallas as pl
from jax.experimental.pallas import tpu as pltpu
from jax.sharding import PartitionSpec as P

BLOCK = 256
EPSILON = 1e-06
F32 = jnp.float32
BF16 = jnp.bfloat16


def plain(a, b):
    return jnp.dot(a, b, preferred_element_type=F32)


def against(a, b):
    return lax.dot_general(a, b, (((1,), (1,)), ((), ())), preferred_element_type=F32)


def outer(a, b):
    return lax.dot_general(a, b, (((0,), (0,)), ((), ())), preferred_element_type=F32)


def column_tiles(count, tile, body):
    whole = count // tile

    if whole:

        @pl.loop(0, whole)
        def _(i):
            body(pl.multiple_of(i * tile, tile), tile)

    if count - whole * tile:
        body(whole * tile, count - whole * tile)


def row_mean(v):
    return jnp.mean(v, axis=-1, keepdims=True)


def valid_rows(scalars, half, rows):
    c, length = scalars[0], scalars[2]
    first = rows * (c if half == 0 else 1 - c)
    return (first + lax.broadcasted_iota(jnp.int32, (rows, 1), 0) < length).astype(F32)


def decays(rate, n):
    i = lax.broadcasted_iota(jnp.int32, (n, n), 0)
    j = lax.broadcasted_iota(jnp.int32, (n, n), 1)
    gap = (i - j).astype(F32)
    mask = jnp.where(gap >= 0, jnp.exp(-rate * jnp.maximum(gap, 0.0)), 0.0)
    step = lax.broadcasted_iota(jnp.int32, (n, 1), 0).astype(F32)
    return mask, jnp.exp(-rate * (step + 1.0)), jnp.exp(-rate * (n - 1.0 - step))


def attention_forward(
    scalars, rates, tok_own, tok_other, w_query, w_key, w_value, w_gate,
    nin, q_out, k_out, v_out, dq_out, dk_out, gu_out, dg_out, att_out, u_out, prior_out,
    gate_buf,
):
    rows = tok_own.shape[0]
    cols = q_out.shape[1]
    c = scalars[0]
    valid = []
    for half, tok in enumerate((tok_own, tok_other)):
        x = tok[...].astype(F32)
        nin[half * rows : (half + 1) * rows, :] = (
            x * lax.rsqrt(row_mean(x * x) + EPSILON)
        ).astype(BF16)
        valid.append(valid_rows(scalars, half, rows))
    for half in (0, 1):
        part = slice(half * rows, (half + 1) * rows)
        ok = valid[half]
        for start in range(0, cols, BLOCK):
            at = slice(start, start + BLOCK)
            normed = nin[part, :]
            pre = plain(normed, w_query[:, at])
            sig = jax.nn.sigmoid(pre)
            act = pre * sig
            q_out[part, at] = act.astype(BF16)
            dq_out[part, at] = (sig + act * (1.0 - sig)).astype(BF16)
            pre = plain(normed, w_key[:, at])
            sig = jax.nn.sigmoid(pre)
            act = pre * sig
            k_out[part, at] = (act * ok).astype(BF16)
            dk_out[part, at] = ((sig + act * (1.0 - sig)) * ok).astype(BF16)
            v_out[part, at] = (plain(normed, w_value[:, at]) * ok).astype(BF16)
            pre = plain(normed, w_gate[:, at])
            sig = jax.nn.sigmoid(pre)
            act = pre * sig
            gate_buf[part, at] = act
            gu_out[part, at] = act.astype(BF16)
            dg_out[part, at] = (sig + act * (1.0 - sig)).astype(BF16)
    size = prior_out.shape[1]
    heads = prior_out.shape[0]
    carried = (scalars[2] > rows).astype(F32)
    first = pl.ds(pl.multiple_of(c * rows, rows), rows)
    second = pl.ds(pl.multiple_of((1 - c) * rows, rows), rows)
    squares = [jnp.zeros((rows, 1), F32), jnp.zeros((rows, 1), F32)]
    for h in range(heads):
        at = slice(h * size, (h + 1) * size)
        mask, query_decay, key_decay = decays(rates[c * heads + h], rows)
        wide = (k_out[first, at].astype(F32) * key_decay).astype(BF16)
        prior = (outer(wide, v_out[first, at]) * carried).astype(BF16)
        prior_out[h] = prior
        for b, part in enumerate((first, second)):
            q = q_out[part, at]
            weighted = (against(q, k_out[part, at]) * mask).astype(BF16)
            att = plain(weighted, v_out[part, at])
            if b == 1:
                att = att + plain(q, prior) * query_decay
            att_out[part, at] = att.astype(BF16)
            u_out[part, at] = (att * gate_buf[part, at]).astype(BF16)
            squares[b] = squares[b] + jnp.sum(att * att, axis=-1, keepdims=True)
    lane = lax.broadcasted_iota(jnp.int32, (rows, 128), 1)
    for b, part in enumerate((first, second)):
        high = squares[b].astype(BF16).astype(F32)
        low = squares[b] - high
        u_out[part, cols:] = jnp.where(lane < 64, high, low).astype(BF16)


def feed_forward(
    scalars, tok_own, tok_other, u_own, u_other, w_out, w_left, w_right, w_down, cot_own, cot_other,
    nm, joined, d_left, d_right, d_ffn, branch_out, scale_out,
):
    rows, width = tok_own.shape
    cols = u_own.shape[1] - 128
    c = scalars[0]
    own = pl.ds(pl.multiple_of(c * cols, cols), cols)
    other = pl.ds(pl.multiple_of((1 - c) * cols, cols), cols)
    for half in (0, 1):
        part = slice(half * rows, (half + 1) * rows)
        swap = slice((1 - half) * rows, (2 - half) * rows)
        total = jnp.zeros((rows, 1), F32)
        for lane in (0, 64):
            total = total + u_own[part, cols + lane : cols + lane + 1].astype(F32)
            total = total + u_other[swap, cols + lane : cols + lane + 1].astype(F32)
        scale = lax.rsqrt(total / width + EPSILON)
        scale_out[part, :] = jnp.broadcast_to(scale, (rows, 128))
        branch = scale * (
            plain(u_own[part, :cols], w_out[own, :]) + plain(u_other[swap, :cols], w_out[other, :])
        )
        branch_out[part, :] = branch.astype(BF16)
        ok = valid_rows(scalars, half, rows)
        hidden = (tok_own, tok_other)[half][...].astype(F32) + ok * branch
        nm[part, :] = (hidden * lax.rsqrt(row_mean(hidden * hidden) + EPSILON)).astype(BF16)
        cot = (cot_own, cot_other)[half][...].astype(F32)
        d_ffn[part, :] = (cot * ok).astype(BF16)

    def body(start, count):
        at = pl.ds(start, count)
        left = plain(nm[...], w_left[:, at])
        right = plain(nm[...], w_right[:, at])
        joined[:, at] = (left * right).astype(BF16)
        d_joined = against(d_ffn[...], w_down[at, :])
        d_left[:, at] = (d_joined * right).astype(BF16)
        d_right[:, at] = (d_joined * left).astype(BF16)

    column_tiles(w_left.shape[1], 256, body)


def place_rows(wide, dims, pos, count):
    mask = 0
    for k, d in enumerate(dims):
        if pos >> (len(dims) - 1 - k) & 1:
            mask |= 1 << d
    return wide ^ mask


def transposed_rows(scalars, source, target, dims, first=0):
    n = 1 << len(dims)
    rows = target.shape[0] // n
    for pos in range(n):
        block = place_rows(scalars[1], dims, pos, n)
        target[pos * rows : (pos + 1) * rows, :] = source[
            pl.ds(pl.multiple_of(block * rows, rows), rows), :
        ]


def outer_products(orders, scalars, *refs):
    count = len(orders)
    lefts, rights = refs[:count], refs[count : 2 * count]
    outs, (flat, placed) = refs[2 * count : 4 * count], refs[4 * count :]
    done = None
    for k, (dims, left) in enumerate(orders):
        if left != done:
            for at in range(0, flat.shape[0], 128):
                flat[at : at + 128, :] = lefts[k][:, at : at + 128].T
            done = left
        transposed_rows(scalars, flat, placed, dims)
        half = flat.shape[0] // 2
        stays, goes, right = outs[2 * k], outs[2 * k + 1], rights[k]

        def body(start, size):
            at = pl.ds(start, size)
            stays[:, at] = plain(placed[:half, :], right[:, at]).astype(BF16)
            goes[:, at] = plain(placed[half:, :], right[:, at]).astype(BF16)

        column_tiles(right.shape[1], 256, body)


def mid_gradient(d_left, d_right, w_left, w_right, out):
    def body(start, count):
        at = pl.ds(start, count)
        total = against(d_left[...], w_left[at, :]) + against(d_right[...], w_right[at, :])
        out[:, at] = total.astype(BF16)

    column_tiles(out.shape[1], 256, body)


def down_projection(joined, w_down, stays, goes):
    rows = stays.shape[0]

    def body(start, count):
        at = pl.ds(start, count)
        total = plain(joined[...], w_down[:, at])
        stays[:, at] = total[:rows]
        goes[:, at] = total[rows:].astype(BF16)

    column_tiles(stays.shape[1], 256, body)


def attention_backward(
    scalars, rates, tok_own, tok_other, cot_own, cot_other, nm, branch, mid_own, mid_other,
    scale_ref, w_out, u_own, u_other, q_ref, k_ref, v_ref, dq_ref, dk_ref, gu_ref, dg_ref, att_ref, prior_ref,
    dpre_q, dpre_k, dpre_v, dpre_g, d_branch, gated, hidden_out,
    d_att,
):
    rows, width = tok_own.shape
    cols = q_ref.shape[1]
    c = scalars[0]
    own = pl.ds(pl.multiple_of(c * cols, cols), cols)
    other = pl.ds(pl.multiple_of((1 - c) * cols, cols), cols)
    for half in (0, 1):
        part = slice(half * rows, (half + 1) * rows)
        swap = slice((1 - half) * rows, (2 - half) * rows)
        ok = valid_rows(scalars, half, rows)
        lined = branch[part, :].astype(F32)
        hidden = (tok_own, tok_other)[half][...].astype(F32) + ok * lined
        mid_scale = lax.rsqrt(row_mean(hidden * hidden) + EPSILON)
        normed = hidden * mid_scale
        d_mid = mid_own[part, :].astype(F32) + mid_other[swap, :].astype(F32)
        d_hidden = (cot_own, cot_other)[half][...].astype(F32) + mid_scale * (
            d_mid - normed * row_mean(d_mid * normed)
        )
        if half == 0:
            hidden_out[...] = d_hidden
        d_out = (ok * d_hidden).astype(BF16)
        d_branch[part, :] = d_out
        inner = row_mean(d_out.astype(F32) * lined)
        scale = scale_ref[part, :1]
        d_gated = against(d_out, w_out[own, :])
        normed = att_ref[part, :].astype(F32) * scale
        dpre_g[part, :] = (d_gated * normed * dg_ref[part, :].astype(F32)).astype(BF16)
        d_att[part, :] = (scale * (d_gated * gu_ref[part, :].astype(F32) - normed * inner)).astype(
            BF16
        )
        gated[part, own] = (u_own[part, :cols].astype(F32) * scale).astype(BF16)
        gated[part, other] = (u_other[swap, :cols].astype(F32) * scale).astype(BF16)
    heads, size = prior_ref.shape[:2]
    carried = (scalars[2] > rows).astype(F32)
    first = pl.ds(pl.multiple_of(c * rows, rows), rows)
    second = pl.ds(pl.multiple_of((1 - c) * rows, rows), rows)
    for h in range(heads):
        at = slice(h * size, (h + 1) * size)
        mask, query_decay, key_decay = decays(rates[c * heads + h], rows)
        prior = prior_ref[h]
        wide = (q_ref[second, at].astype(F32) * query_decay).astype(BF16)
        state = (outer(wide, d_att[second, at]) * carried).astype(BF16)
        for b, part in enumerate((first, second)):
            q, k, v, d_o = q_ref[part, at], k_ref[part, at], v_ref[part, at], d_att[part, at]
            weighted = (against(q, k) * mask).astype(BF16)
            d_scores = (against(d_o, v) * mask).astype(BF16)
            d_q = plain(d_scores, k)
            d_k = outer(d_scores, q)
            d_v = outer(weighted, d_o)
            if b == 1:
                d_q = d_q + against(d_o, prior) * query_decay
            else:
                d_k = d_k + against(v, state) * key_decay
                d_v = d_v + plain(k, state) * key_decay
            ok = jnp.where(
                b * rows + lax.broadcasted_iota(jnp.int32, (rows, 1), 0) < scalars[2], 1.0, 0.0
            )
            dpre_q[part, at] = (d_q * dq_ref[part, at].astype(F32)).astype(BF16)
            dpre_k[part, at] = (d_k * dk_ref[part, at].astype(F32)).astype(BF16)
            dpre_v[part, at] = (d_v * ok).astype(BF16)


def input_gradient(
    dpre_q, dpre_k, dpre_v, dpre_g, w_query, w_key, w_value, w_gate, stays, goes
):
    rows = stays.shape[0]

    def body(start, count):
        at = pl.ds(start, count)
        total = against(dpre_q[...], w_query[at, :]) + against(dpre_k[...], w_key[at, :])
        total += against(dpre_v[...], w_value[at, :]) + against(dpre_g[...], w_gate[at, :])
        stays[:, at] = total[:rows]
        goes[:, at] = total[rows:].astype(BF16)

    column_tiles(stays.shape[1], 256, body)


def finish_input(tok, d_hidden, stays, came, out):
    x = tok[...].astype(F32)
    scale = lax.rsqrt(row_mean(x * x) + EPSILON)
    normed = x * scale
    d_in = stays[...] + came[...].astype(F32)
    out[...] = d_hidden[...] + scale * (d_in - normed * row_mean(d_in * normed))


WHOLE = pl.BlockSpec(memory_space=pltpu.VMEM)
SCALAR = pl.BlockSpec(memory_space=pltpu.SMEM)


def call(body, outs, args, specs=None, scratch=(), scalars=None, name=None):
    specs = specs or {}

    def whole(shape):
        return pl.BlockSpec(shape, lambda i, s: (0,) * len(shape))

    in_specs = [specs.get(i, whole(a.shape)) for i, a in enumerate(args)]
    nbytes = sum(a.size * a.dtype.itemsize for a in args)
    return pl.pallas_call(
        body,
        grid_spec=pltpu.PrefetchScalarGridSpec(
            num_scalar_prefetch=1,
            grid=(1,),
            in_specs=in_specs,
            out_specs=[whole(o.shape) for o in outs],
            scratch_shapes=list(scratch),
        ),
        out_shape=outs,
        name=name,
        compiler_params=pltpu.CompilerParams(vmem_limit_bytes=60 * 1024 * 1024),
    )(scalars, *args)


def arr(shape, dtype=BF16):
    return jax.ShapeDtypeStruct(shape, dtype)


def flipped(n, bit):
    return [(i, i ^ (1 << bit)) for i in range(n)]


def halve(stays, goes, n, bit, last=False):
    came = lax.ppermute(goes, "wide", flipped(n, bit))
    total = stays.astype(F32) + came.astype(F32)
    if last:
        return total
    half = total.shape[0] // 2
    return total[:half].astype(BF16), total[half:].astype(BF16)


def scatter_sums(pairs, orders, n):
    pairs = list(pairs)
    for phase in range(len(orders[0])):
        last = phase == len(orders[0]) - 1
        pairs = [halve(*p, n, dims[phase], last) for p, dims in zip(pairs, orders)]
    return pairs


def on_device(
    tokens,
    seq_lens,
    decay_rate,
    w_query,
    w_key,
    w_value,
    w_gate_u,
    w_out,
    w_left,
    w_right,
    w_down,
    cotangent,
):
    n_wide = lax.axis_size("wide")
    bits = n_wide.bit_length() - 1
    order_x = [0, 1] + list(range(2, bits))
    order_y = [1, 0] + list(range(2, bits))
    order_z = [2, 0, 1] + list(range(3, bits))
    rows, width = tokens.shape
    hidden = w_left.shape[1]
    heads = decay_rate.shape[0] // 2
    size = width // decay_rate.shape[0]
    cols = width // 2
    c = lax.axis_index("narrow")
    wide = lax.axis_index("wide")
    scalars = jnp.stack([c, wide, seq_lens[0, 0]]).astype(jnp.int32)
    swap = [(0, 1), (1, 0)]

    def other(v):
        return lax.ppermute(v, "narrow", swap)

    run = functools.partial(call, scalars=scalars)
    tok_other = other(tokens)
    cot_other = other(cotangent)
    half_cols = pl.BlockSpec((width, cols), lambda i, s: (0, s[0]))
    nin, q, k, v, dq, dk, gu, dg, att, u, prior = run(
        attention_forward,
        [arr((2 * rows, width))]
        + [arr((2 * rows, cols))] * 8
        + [arr((2 * rows, cols + 128)), arr((heads, size, size))],
        (decay_rate, tokens, tok_other, w_query, w_key, w_value, w_gate_u),
        specs={0: SCALAR, 3: half_cols, 4: half_cols, 5: half_cols, 6: half_cols},
        scratch=[pltpu.VMEM((2 * rows, cols), F32)],
        name="attention_forward",
    )
    u_other = other(u)
    nm, joined, d_left, d_right, d_ffn, branch, scale = run(
        feed_forward,
        [arr((2 * rows, width))]
        + [arr((2 * rows, hidden))] * 3
        + [arr((2 * rows, width))] * 2
        + [arr((2 * rows, 128), F32)],
        (tokens, tok_other, u, u_other, w_out, w_left, w_right, w_down, cotangent, cot_other),
        name="feed_forward",
    )

    def products(lefts, rights, which, orders, name):
        half = arr((width // 2, rights[0].shape[1]))
        flat = run(
            functools.partial(outer_products, list(zip(orders, which))),
            [half] * (2 * len(rights)),
            tuple(lefts[i] for i in which) + tuple(rights),
            scratch=[pltpu.VMEM((width, 2 * rows), BF16)] * 2,
            name=name,
        )
        return list(zip(flat[0::2], flat[1::2]))

    pairs = products([d_ffn], [joined], [0], [order_z], "grad_down")
    pairs += products([nm], [d_left, d_right], [0, 0], [order_x, order_y], "grad_left_right")
    grad_down, grad_left, grad_right = scatter_sums(pairs, [order_z, order_x, order_y], n_wide)
    (mid,) = run(
        lambda s, *r: mid_gradient(*r),
        [arr((2 * rows, width))],
        (d_left, d_right, w_left, w_right),
        name="mid_gradient",
    )
    mid_other = other(mid)
    ffn_stays, ffn_goes = run(
        lambda s, *r: down_projection(*r),
        [arr((rows, width), F32), arr((rows, width))],
        (joined, w_down),
        name="down_projection",
    )
    ffn_came = other(ffn_goes)
    dpre_q, dpre_k, dpre_v, dpre_g, d_branch, gated, d_hidden = run(
        attention_backward,
        [arr((2 * rows, cols))] * 4 + [arr((2 * rows, width))] * 2 + [arr((rows, width), F32)],
        (decay_rate, tokens, tok_other, cotangent, cot_other, nm, branch, mid, mid_other)
        + (scale, w_out, u, u_other, q, k, v, dq, dk, gu, dg, att, prior),
        specs={0: SCALAR},
        scratch=[pltpu.VMEM((2 * rows, cols), BF16)],
        name="attention_backward",
    )
    pairs = products(
        [nin],
        [dpre_q, dpre_k, dpre_v, dpre_g],
        [0] * 4,
        [order_x, order_x, order_y, order_y],
        "grad_attention",
    )
    d_mine = lax.dynamic_slice_in_dim(d_branch, c * cols, cols, 1)
    pairs += products([gated], [d_mine], [0], [order_z], "grad_out")
    sums = scatter_sums(pairs, [order_x, order_x, order_y, order_y, order_z], n_wide)
    in_stays, in_goes = run(
        lambda s, *r: input_gradient(*r),
        [arr((rows, width), F32), arr((rows, width))],
        (dpre_q, dpre_k, dpre_v, dpre_g, w_query, w_key, w_value, w_gate_u),
        specs={4: half_cols, 5: half_cols, 6: half_cols, 7: half_cols},
        name="input_gradient",
    )
    (input_grad,) = run(
        lambda s, *r: finish_input(*r),
        [arr((rows, width), F32)],
        (tokens, d_hidden, in_stays, other(in_goes)),
        name="finish_input",
    )
    valid = (c * rows + jnp.arange(rows) < seq_lens[0, 0]).astype(F32)[:, None]
    mixed = (
        tokens.astype(F32)
        + valid * (branch[:rows].astype(F32) + ffn_stays + ffn_came.astype(F32))
    ).astype(BF16)
    stacked = jnp.stack(sums)
    theirs = other(stacked)
    both = jnp.where(
        c == 0,
        jnp.concatenate([stacked, theirs], axis=2),
        jnp.concatenate([theirs, stacked], axis=2),
    )
    return (
        mixed,
        input_grad,
        both[0],
        both[1],
        both[2],
        both[3],
        both[4],
        grad_left,
        grad_right,
        grad_down.T,
    )


def solution(mesh):
    placed = (
        P(("wide", "narrow"), None),
        P("wide", None),
        P(),
        P(),
        P(),
        P(),
        P(),
        P(),
        P(None, "narrow"),
        P(None, "narrow"),
        P("narrow", None),
        P(("wide", "narrow"), None),
    )
    return jax.shard_map(
        on_device,
        mesh=mesh,
        in_specs=placed,
        out_specs=(
            P(("wide", "narrow"), None),
            P(("wide", "narrow"), None),
            P("wide", None),
            P("wide", None),
            P("wide", None),
            P("wide", None),
            P("wide", None),
            P("wide", "narrow"),
            P("wide", "narrow"),
            P("narrow", "wide"),
        ),
        check_vma=False,
    )
```

time: 1030 us -> 275 us (0.27)
  waiting for transfers between devices: 852 us -> 108 us
  matrix products: 99.4 us -> 0 us
  Pallas kernels: 0 us -> 96.3 us
  starting transfers between devices: 5.63 us -> 38.2 us
  local copies, waits for them, and re-layouts: 31.8 us -> 13.2 us
  between operations: 16.9 us -> 1.79 us
    reduce_scatter x10 -> x0, waiting for transfers between devices: 814 us -> none  [the longest x1 130 us: on_device(): lax.psum_scatter(grad_right, 'wide', scatter_dimension=0, tiled=True)]
    ppermute x2 -> x39, waiting for transfers between devices: 0.01 us -> 108 us  [the longest x32 105 us: halve(): came = lax.ppermute(goes, 'wide', flipped(n, bit))]
    dot_general x36 -> x0, matrix products: 99.4 us -> none  [the longest x8 32.3 us: dot_outer(): lax.dot_general(left_side, right_side, (((0,), (0,)), ((), ())), preferre...]
    pallas_call x0 -> x11, Pallas kernels: none -> 96.3 us  [call(): pl.pallas_call(body, grid_spec=pltpu.PrefetchScalarGridSpec(num_scalar_pr...]
    ppermute x2 -> x39, starting transfers between devices: 4.46 us -> 38.2 us  [the longest x32 36.5 us: halve(): came = lax.ppermute(goes, 'wide', flipped(n, bit))]
    psum x1 -> x0, waiting for transfers between devices: 24 us -> none  [on_device(): lax.psum((grad_query, grad_key, grad_value, grad_gate_u, grad_out), 'narr...]
    unnamed x99 -> x48, local copies, waits for them, and re-layouts: 20.2 us -> 3.63 us
    all_gather x2 -> x0, waiting for transfers between devices: 13.1 us -> none  [the longest x1 10.3 us: on_device(): mid_rows = lax.all_gather(normed_mid, 'narrow', axis=0, tiled=True)]
  transfers between devices with their start and end apart: 15 -> 39, of which waited for: 13 -> 20; matrix products, arithmetic and copies ran while one was open for 9% -> 9% of each run, Pallas kernels for 0% -> 24%
where the time goes in v1:
time: 275 us; the launch traced here: 274 us
  waiting for transfers between devices  108 us (39%)
  Pallas kernels  96.3 us (35%)
  starting transfers between devices  38.2 us (14%)
  other arithmetic  16.7 us (6%)
  local copies, waits for them, and re-layouts  13.2 us (5%)
    ppermute x32, waiting for transfers between devices, halve(): came = lax.ppermute(goes, 'wide', flipped(n, bit))  105 us
    pallas_call x11, Pallas kernels, call(): pl.pallas_call(body, grid_spec=pltpu.PrefetchScalarGridSpec(num_scalar_pr...  96.3 us
    ppermute x32, starting transfers between devices, halve(): came = lax.ppermute(goes, 'wide', flipped(n, bit))  36.5 us
    another operation x24, other arithmetic  11.3 us
    slice x24, local copies, waits for them, and re-layouts, halve(): return (total[:half].astype(BF16), total[half:].astype(BF16))  6.59 us
  transfers between devices with their start and end apart: 39, of which 20 were waited for; matrix products, arithmetic and copies ran while one was open for 9% of the time, Pallas kernels for 24%

profile of v1, /device:TPU:0, one launch (start us, length us, event | category | flops | bytes accessed | tf_op | source)
XLA Modules:
  0.0 274.2 jit_solution(15760588485044131212)
XLA Ops:
  2.9 0.8 copy-done.3
  3.7 8.6 %attention_forward.1 = (bf16[512,1024]{1,0:T(8,128)(2,1)}, bf16[512,512]{1,0:T(8,128)(2,1)}, bf16[512,512]{1,0:T(8,128)(2,1)}, bf16[512,512]{1,0:T(8,128)(2,1)},...) custom-call(s32[3]{0:T(128)} %pad_add_fusion.scalars.s, ...), custom_call_target="tpu_custom_call" | custom-call | tf_op jit(solution)/shard_map/attention_forward/pallas_call | solution.py:329
  12.8 2.3 collective-permute-done.2.cot_other
  15.2 0.8 copy-done.7
  16.0 0.8 copy-done.4
  16.8 15.7 %feed_forward.1 = (bf16[512,1024]{1,0:T(8,128)(2,1)}, bf16[512,1408]{1,0:T(8,128)(2,1)}, bf16[512,1408]{1,0:T(8,128)(2,1)}, bf16[512,1408]{1,0:T(8,128)(2,1)}, b...) custom-call(s32[3]{0:T(128)} %pad_add_fusion.scalars.s, bf16[256,1024]{1,0:T(8,128)(2,1)} %r_0_.1, ...), custom_call_target="tpu_custom_call" | custom-call | tf_op jit(solution)/shard_map/feed_forward/pallas_call | solution.py:329
  32.5 6.9 %grad_down.1 = (bf16[512,1408]{1,0:T(8,128)(2,1)}, bf16[512,1408]{1,0:T(8,128)(2,1)}) custom-call(s32[3]{0:T(128)} %pad_add_fusion.scalars.s, bf16[512,1024]{1,0:T(8,128)(2,1)} %get-tuple-element.97.refs_0_, bf16[512,1408]{1,0:T(8,128)(2,1)} %get-tuple-element.57.r_0_.refs_1_), custom_call_target="tpu_custom_call" | custom-call | tf_op jit(solution)/shard_map/grad_down/pallas_call | solution.py:329
  39.4 3.0 %collective-permute-start.35 = (bf16[512,1408]{1,0:T(8,128)(2,1)}, bf16[512,1408]{1,0:T(8,128)(2,1)S(1)}, u32[]{:S(2)}, u32[]{:S(2)}) collective-permute-start(bf16[512,1408]{1,0:T(8,128)(2,1)} %get-tuple-element.99), channel_id=1, source_target_pairs={{0,8},{2,10},{4,12},{6,14},{8,0},{10,2},{12,4},{14,6},{16,24},{18,... | collective-permute-start | bytes 4325384 | tf_op jit(solution)/shard_map/ppermute | solution.py:353
  42.4 9.1 %mid_gradient.1.mid_own = bf16[512,1024]{1,0:T(8,128)(2,1)} custom-call(s32[3]{0:T(128)} %pad_add_fusion.scalars.s, bf16[512,1408]{1,0:T(8,128)(2,1)} %get-tuple-element.61.r_0_.refs_2_, bf16[512,1408]{1,0:T(8,128)(2,1)} %get-tuple-element.62.r_1_.refs_3_, bf16[1024,1408]{1,0:T(8,128)(2,1)} %r_2_.1, bf16[1024,1408]{1,0:T(8,128)(2,1)} %r_3_.1), custom_call_target="tpu_custom_call" | custom-call | tf_op jit(solution)/shard_map/mid_gradient/pallas_call | solution.py:329
  51.5 6.4 %down_projection.1 = (f32[256,1024]{1,0:T(8,128)}, bf16[256,1024]{1,0:T(8,128)(2,1)}) custom-call(s32[3]{0:T(128)} %pad_add_fusion.scalars.s, bf16[512,1408]{1,0:T(8,128)(2,1)} %get-tuple-element.57.r_0_.refs_1_, bf16[1408,1024]{1,0:T(8,128)(2,1)} %r_1_.1), custom_call_target="tpu_custom_call" | custom-call | tf_op jit(solution)/shard_map/down_projection/pallas_call | solution.py:329
  58.4 10.7 %grad_left_right.1 = (bf16[512,1408]{1,0:T(8,128)(2,1)}, bf16[512,1408]{1,0:T(8,128)(2,1)}, bf16[512,1408]{1,0:T(8,128)(2,1)}, bf16[512,1408]{1,0:T(8,128)(2,1)}) custom-call(s32[3]{0:T(128)} %pad_add_fusion.scalars.s, bf16[512,1024]{1,0:T(8,128)(2,1)} %get-tuple-element.60.nm.refs_0_.refs_1_, bf16[512,1024]{1,0:T(8,128)(2,1)} %get-tuple-element.60.nm.refs_0_.refs_1_, ...), custom_call_target="tpu_custom_call" | custom-call | tf_op jit(solution)/shard_map/grad_left_right/pallas_call | solution.py:329
  69.0 1.5 collective-permute-start.31
  70.6 1.5 collective-permute-start.27
  72.1 2.3 add_convert_fusion.11
  74.3 13.6 %attention_backward.1 = (bf16[512,512]{1,0:T(8,128)(2,1)}, bf16[512,512]{1,0:T(8,128)(2,1)}, bf16[512,512]{1,0:T(8,128)(2,1)}, bf16[512,512]{1,0:T(8,128)(2,1)},...) custom-call(s32[3]{0:T(128)} %pad_add_fusion.scalars.s, f32[8]{0:T(128)} %rates.3, ...), custom_call_target="tpu_custom_call" | custom-call | tf_op jit(solution)/shard_map/attention_backward/pallas_call | solution.py:329
  88.0 1.9 constant_dynamic-slice_fusion.refs_1_
  89.8 4.3 %grad_out.1 = (bf16[512,512]{1,0:T(8,128)(2,1)}, bf16[512,512]{1,0:T(8,128)(2,1)}) custom-call(s32[3]{0:T(128)} %pad_add_fusion.scalars.s, bf16[512,1024]{1,0:T(8,128)(2,1)} %get-tuple-element.89.refs_0_, bf16[512,512]{1,0:T(8,128)(2,1)} %constant_dynamic-slice_fusion.refs_1_), custom_call_target="tpu_custom_call" | custom-call | tf_op jit(solution)/shard_map/grad_out/pallas_call | solution.py:329
  94.6 7.5 %input_gradient.1 = (f32[256,1024]{1,0:T(8,128)}, bf16[256,1024]{1,0:T(8,128)(2,1)}) custom-call(s32[3]{0:T(128)} %pad_add_fusion.scalars.s, bf16[512,512]{1,0:T(8,128)(2,1)} %get-tuple-element.74.r_0_.refs_4_, bf16[512,512]{1,0:T(8,128)(2,1)} %get-tuple-element.75.r_1_.refs_5_, bf16[512,512]{1,0:T(8,128)(2,1)} %get-tuple-element.76.r_2_.refs_6_, ...), custom_call_target="tpu_custom_call" | custom-call | tf_op jit(solution)/shard_map/input_gradient/pallas_call | solution.py:329
  102.1 9.6 %grad_attention.1 = (bf16[512,512]{1,0:T(8,128)(2,1)}, bf16[512,512]{1,0:T(8,128)(2,1)}, bf16[512,512]{1,0:T(8,128)(2,1)}, bf16[512,512]{1,0:T(8,128)(2,1)}, bf1...) custom-call(s32[3]{0:T(128)} %pad_add_fusion.scalars.s, ...), custom_call_target="tpu_custom_call" | custom-call | tf_op jit(solution)/shard_map/grad_attention/pallas_call | solution.py:329
  112.3 1.5 collective-permute-start.14
  115.8 1.8 add_convert_fusion.1
  117.7 1.1 collective-permute-start.6
  118.8 1.7 add_convert_fusion.2
  120.5 0.9 slice.312
  121.4 0.9 slice.306
  122.4 0.9 slice.300
  124.2 2.6 collective-permute-done.18
  128.2 7.9 %collective-permute-done.14 = bf16[512,512]{1,0:T(8,128)(2,1)S(1)} collective-permute-done((bf16[512,512]{1,0:T(8,128)(2,1)}, bf16[512,512]{1,0:T(8,128)(2,1)S(1)}, u32[]{:S(2)}, u32[]{:S(2)}) %collective-permute-start.14) | collective-permute-done | bytes 524320 | tf_op jit(solution)/shard_map/ppermute | solution.py:353
  136.9 1.5 collective-permute-start.23
  138.6 2.3 collective-permute-done.6
  143.8 3.9 %finish_input.1 = f32[256,1024]{1,0:T(8,128)} custom-call(s32[3]{0:T(128)} %pad_add_fusion.scalars.s, bf16[256,1024]{1,0:T(8,128)(2,1)} %r_0_.1, f32[256,1024]{1,0:T(8,128)} %get-tuple-element.73.r_1_, f32[256,1024]{1,0:T(8,128)} %get-tuple-element.78.r_2_, bf16[256,1024]{1,0:T(8,128)(2,1)} %collective-permute-done.5.r_3_), custom_call_target="tpu_custom_call" | custom-call | tf_op jit(solution)/shard_map/finish_input/pallas_call | solution.py:329
  147.8 29.7 %collective-permute-done.23 = bf16[256,512]{1,0:T(8,128)(2,1)} collective-permute-done((bf16[256,512]{1,0:T(8,128)(2,1)}, bf16[256,512]{1,0:T(8,128)(2,1)}, u32[]{:S(2)}, u32[]{:S(2)}) %collective-permute-start.23) | collective-permute-done | bytes 262176 | tf_op jit(solution)/shard_map/ppermute | solution.py:353
  178.1 1.1 add_convert_fusion.15
  179.2 4.0 %collective-permute-done.19 = bf16[256,512]{1,0:T(8,128)(2,1)} collective-permute-done((bf16[256,512]{1,0:T(8,128)(2,1)}, bf16[256,512]{1,0:T(8,128)(2,1)}, u32[]{:S(2)}, u32[]{:S(2)}) %collective-permute-start.19) | collective-permute-done | bytes 262176 | tf_op jit(solution)/shard_map/ppermute | solution.py:353
  183.7 1.1 add_convert_fusion.16
  184.8 1.4 collective-permute-done.15
  186.9 5.6 %collective-permute-done.11 = bf16[256,512]{1,0:T(8,128)(2,1)S(1)} collective-permute-done((bf16[256,512]{1,0:T(8,128)(2,1)}, bf16[256,512]{1,0:T(8,128)(2,1)S(1)}, u32[]{:S(2)}, u32[]{:S(2)}) %collective-permute-start.11) | collective-permute-done | bytes 262176 | tf_op jit(solution)/shard_map/ppermute | solution.py:353
  193.1 3.2 %collective-permute-done.7 = bf16[256,512]{1,0:T(8,128)(2,1)S(1)} collective-permute-done((bf16[256,512]{1,0:T(8,128)(2,1)S(1)}, bf16[256,512]{1,0:T(8,128)(2,1)S(1)}, u32[]{:S(2)}, u32[]{:S(2)}) %collective-permute-start.7) | collective-permute-done | bytes 262176 | tf_op jit(solution)/shard_map/ppermute | solution.py:353
  196.3 1.6 collective-permute-start.20
  198.0 1.3 collective-permute-start.8
  199.3 5.1 %collective-permute-done.8 = bf16[128,512]{1,0:T(8,128)(2,1)S(1)} collective-permute-done((bf16[128,512]{1,0:T(8,128)(2,1)S(1)}, bf16[128,512]{1,0:T(8,128)(2,1)S(1)}, u32[]{:S(2)}, u32[]{:S(2)}) %collective-permute-start.8) | collective-permute-done | bytes 131104 | tf_op jit(solution)/shard_map/ppermute | solution.py:353
  204.4 1.5 collective-permute-start.16
  206.6 3.0 %collective-permute-done.16 = bf16[128,512]{1,0:T(8,128)(2,1)S(1)} collective-permute-done((bf16[128,512]{1,0:T(8,128)(2,1)S(1)}, bf16[128,512]{1,0:T(8,128)(2,1)S(1)}, u32[]{:S(2)}, u32[]{:S(2)}) %collective-permute-start.16) | collective-permute-done | bytes 131104 | tf_op jit(solution)/shard_map/ppermute | solution.py:353
  209.6 2.8 %collective-permute-start.25 = (bf16[64,512]{1,0:T(8,128)(2,1)S(1)}, bf16[64,512]{1,0:T(8,128)(2,1)S(1)}, u32[]{:S(2)}, u32[]{:S(2)}) collective-permute-start(bf16[64,512]{1,0:T(8,128)(2,1)S(1)} %slice.293), channel_id=1, source_target_pairs={{0,16},{2,18},{4,20},{6,22},{8,24},{10,26},{12,28},{14,30},{16,0},... | collective-permute-start | bytes 196616 | tf_op jit(solution)/shard_map/ppermute | solution.py:353
  212.5 1.5 collective-permute-start.9
  214.1 3.6 %collective-permute-done.9 = bf16[64,512]{1,0:T(8,128)(2,1)S(1)} collective-permute-done((bf16[64,512]{1,0:T(8,128)(2,1)S(1)}, bf16[64,512]{1,0:T(8,128)(2,1)S(1)}, u32[]{:S(2)}, u32[]{:S(2)}) %collective-permute-start.9) | collective-permute-done | bytes 65568 | tf_op jit(solution)/shard_map/ppermute | solution.py:353
  217.7 1.6 collective-permute-start.13
  219.3 3.6 %collective-permute-done.13 = bf16[64,512]{1,0:T(8,128)(2,1)S(1)} collective-permute-done((bf16[64,512]{1,0:T(8,128)(2,1)S(1)}, bf16[64,512]{1,0:T(8,128)(2,1)S(1)}, u32[]{:S(2)}, u32[]{:S(2)}) %collective-permute-start.13) | collective-permute-done | bytes 65568 | tf_op jit(solution)/shard_map/ppermute | solution.py:353
  222.9 1.7 collective-permute-start.17
  224.6 3.7 %collective-permute-done.17 = bf16[64,512]{1,0:T(8,128)(2,1)S(1)} collective-permute-done((bf16[64,512]{1,0:T(8,128)(2,1)S(1)}, bf16[64,512]{1,0:T(8,128)(2,1)S(1)}, u32[]{:S(2)}, u32[]{:S(2)}) %collective-permute-start.17) | collective-permute-done | bytes 65568 | tf_op jit(solution)/shard_map/ppermute | solution.py:353
  228.3 1.5 collective-permute-start.21
  229.9 3.6 %collective-permute-done.21 = bf16[64,512]{1,0:T(8,128)(2,1)S(1)} collective-permute-done((bf16[64,512]{1,0:T(8,128)(2,1)S(1)}, bf16[64,512]{1,0:T(8,128)(2,1)S(1)}, u32[]{:S(2)}, u32[]{:S(2)}) %collective-permute-start.21) | collective-permute-done | bytes 65568 | tf_op jit(solution)/shard_map/ppermute | solution.py:353
  233.7 1.3 add_convert_fusion.3
  235.3 1.3 add_convert_fusion.4
  236.7 2.4 collective-permute-start.33
  239.1 1.3 add_convert_fusion.5
  240.5 5.4 %collective-permute-done.37 = bf16[128,1408]{1,0:T(8,128)(2,1)S(1)} collective-permute-done((bf16[128,1408]{1,0:T(8,128)(2,1)S(1)}, bf16[128,1408]{1,0:T(8,128)(2,1)S(1)}, u32[]{:S(2)}, u32[]{:S(2)}) %collective-permute-start.37) | collective-permute-done | bytes 360480 | tf_op jit(solution)/shard_map/ppermute | solution.py:353
  246.0 1.6 collective-permute-start.38
  248.4 2.4 collective-permute-start.34
  250.8 12.5 %collective-permute-done.29 = bf16[128,1408]{1,0:T(8,128)(2,1)S(1)} collective-permute-done((bf16[128,1408]{1,0:T(8,128)(2,1)S(1)}, bf16[128,1408]{1,0:T(8,128)(2,1)S(1)}, u32[]{:S(2)}, u32[]{:S(2)}) %collective-permute-start.29) | collective-permute-done | bytes 360480 | tf_op jit(solution)/shard_map/ppermute | solution.py:353
  263.7 1.1 slice_bitcast_fusion
  264.8 0.8 add_bitcast_fusion
  265.6 0.8 convert_add_fusion
  266.3 7.0 %collective-permute-done.30 = bf16[64,1408]{1,0:T(8,128)(2,1)S(1)} collective-permute-done((bf16[64,1408]{1,0:T(8,128)(2,1)S(1)}, bf16[64,1408]{1,0:T(8,128)(2,1)S(1)}, u32[]{:S(2)}, u32[]{:S(2)}) %collective-permute-start.30) | collective-permute-done | bytes 180256 | tf_op jit(solution)/shard_map/ppermute | solution.py:353
  (135 shorter events, 17.8 us)
Async XLA Ops:
  0.6 2.3 collective-permute-start
  2.4 10.3 %copy-start.6 = (bf16[256,1024]{1,0:T(8,128)(2,1)S(1)}, bf16[256,1024]{1,0:T(8,128)(2,1)}, u32[]{:S(2)}) copy-start(bf16[256,1024]{1,0:T(8,128)(2,1)} %cot_own.3) | copy-start | bytes 1572868
  2.9 0.8 copy-start.3
  12.3 2.9 %collective-permute-start.1 = (bf16[512,640]{1,0:T(8,128)(2,1)}, bf16[512,640]{1,0:T(8,128)(2,1)S(1)}, u32[]{:S(2)}, u32[]{:S(2)}) collective-permute-start(bf16[512,640]{1,0:T(8,128)(2,1)} %get-tuple-element.55.u_own), channel_id=1, source_target_pairs={{0,1},{1,0},{2,3},{3,2},{4,5},{5,4},{6,7},{7,6},{8,9},{9,8},{10,11... | collective-permute-start | bytes 1966088 | tf_op jit(solution)/shard_map/ppermute | solution.py:399
  12.7 2.5 collective-permute-start.2
  15.2 0.8 copy-start.7
  15.9 0.8 copy-start.4
  39.4 72.9 %collective-permute-start.35 = (bf16[512,1408]{1,0:T(8,128)(2,1)}, bf16[512,1408]{1,0:T(8,128)(2,1)S(1)}, u32[]{:S(2)}, u32[]{:S(2)}) collective-permute-start(bf16[512,1408]{1,0:T(8,128)(2,1)} %get-tuple-element.99), channel_id=1, source_target_pairs={{0,8},{2,10},{4,12},{6,14},{8,0},{10,2},{12,4},{14,6},{16,24},{18,... | collective-permute-start | bytes 4325384 | tf_op jit(solution)/shard_map/ppermute | solution.py:353
  51.5 22.9 %collective-permute-start.4 = (bf16[512,1024]{1,0:T(8,128)(2,1)}, bf16[512,1024]{1,0:T(8,128)(2,1)}, u32[]{:S(2)}, u32[]{:S(2)}) collective-permute-start(bf16[512,1024]{1,0:T(8,128)(2,1)} %mid_gradient.1.mid_own), channel_id=1, source_target_pairs={{0,1},{1,0},{2,3},{3,2},{4,5},{5,4},{6,7},{7,6},{8,9},{9,8},{10,11... | collective-permute-start | bytes 3145736 | tf_op jit(solution)/shard_map/ppermute | solution.py:399
  57.9 14.2 %collective-permute-start.3 = (bf16[256,1024]{1,0:T(8,128)(2,1)}, bf16[256,1024]{1,0:T(8,128)(2,1)S(1)}, u32[]{:S(2)}, u32[]{:S(2)}) collective-permute-start(bf16[256,1024]{1,0:T(8,128)(2,1)} %get-tuple-element.59), channel_id=1, source_target_pairs={{0,1},{1,0},{2,3},{3,2},{4,5},{5,4},{6,7},{7,6},{8,9},{9,8},{10,11... | collective-permute-start | bytes 1572872 | tf_op jit(solution)/shard_map/ppermute | solution.py:399
  58.4 13.7 %copy-start = (bf16[256,1024]{1,0:T(8,128)(2,1)S(1)}, bf16[256,1024]{1,0:T(8,128)(2,1)}, u32[]{:S(2)}) copy-start(bf16[256,1024]{1,0:T(8,128)(2,1)} %r_0_.1) | copy-start | bytes 1572868
  58.4 13.7 %copy-start.5 = (bf16[512,1024]{1,0:T(8,128)(2,1)S(1)}, bf16[512,1024]{1,0:T(8,128)(2,1)}, u32[]{:S(2)}) copy-start(bf16[512,1024]{1,0:T(8,128)(2,1)} %get-tuple-element.56.branch) | copy-start | bytes 3145732
  69.0 45.1 %collective-permute-start.31 = (bf16[512,1408]{1,0:T(8,128)(2,1)}, bf16[512,1408]{1,0:T(8,128)(2,1)}, u32[]{:S(2)}, u32[]{:S(2)}) collective-permute-start(bf16[512,1408]{1,0:T(8,128)(2,1)} %get-tuple-element.96), channel_id=1, source_target_pairs={{0,4},{2,6},{4,0},{6,2},{8,12},{10,14},{12,8},{14,10},{16,20},{18,... | collective-permute-start | bytes 4325384 | tf_op jit(solution)/shard_map/ppermute | solution.py:353
  70.6 47.1 %collective-permute-start.27 = (bf16[512,1408]{1,0:T(8,128)(2,1)}, bf16[512,1408]{1,0:T(8,128)(2,1)}, u32[]{:S(2)}, u32[]{:S(2)}) collective-permute-start(bf16[512,1408]{1,0:T(8,128)(2,1)} %get-tuple-element.94), channel_id=1, source_target_pairs={{0,2},{2,0},{4,6},{6,4},{8,10},{10,8},{12,14},{14,12},{16,18},{18,... | collective-permute-start | bytes 4325384 | tf_op jit(solution)/shard_map/ppermute | solution.py:353
  94.1 29.2 %collective-permute-start.22 = (bf16[512,512]{1,0:T(8,128)(2,1)}, bf16[512,512]{1,0:T(8,128)(2,1)S(1)}, u32[]{:S(2)}, u32[]{:S(2)}) collective-permute-start(bf16[512,512]{1,0:T(8,128)(2,1)} %get-tuple-element.92), channel_id=1, source_target_pairs={{0,8},{2,10},{4,12},{6,14},{8,0},{10,2},{12,4},{14,6},{16,24},{18,... | collective-permute-start | bytes 1572872 | tf_op jit(solution)/shard_map/ppermute | solution.py:353
  102.1 11.6 %copy-start.12 = (bf16[512,1408]{1,0:T(8,128)(2,1)S(1)}, bf16[512,1408]{1,0:T(8,128)(2,1)}, u32[]{:S(2)}) copy-start(bf16[512,1408]{1,0:T(8,128)(2,1)} %get-tuple-element.98) | copy-start | bytes 4325380
  111.7 15.1 %collective-permute-start.18 = (bf16[512,512]{1,0:T(8,128)(2,1)}, bf16[512,512]{1,0:T(8,128)(2,1)S(1)}, u32[]{:S(2)}, u32[]{:S(2)}) collective-permute-start(bf16[512,512]{1,0:T(8,128)(2,1)} %get-tuple-element.88), channel_id=1, source_target_pairs={{0,4},{2,6},{4,0},{6,2},{8,12},{10,14},{12,8},{14,10},{16,20},{18,... | collective-permute-start | bytes 1572872 | tf_op jit(solution)/shard_map/ppermute | solution.py:353
  112.3 23.9 %collective-permute-start.14 = (bf16[512,512]{1,0:T(8,128)(2,1)}, bf16[512,512]{1,0:T(8,128)(2,1)S(1)}, u32[]{:S(2)}, u32[]{:S(2)}) collective-permute-start(bf16[512,512]{1,0:T(8,128)(2,1)} %get-tuple-element.86), channel_id=1, source_target_pairs={{0,4},{2,6},{4,0},{6,2},{8,12},{10,14},{12,8},{14,10},{16,20},{18,... | collective-permute-start | bytes 1572872 | tf_op jit(solution)/shard_map/ppermute | solution.py:353
  113.8 1.0 copy-start.23
  113.8 2.0 copy-start.14
  114.1 6.4 %copy-start.1 = (bf16[512,1408]{1,0:T(8,128)(2,1)}, bf16[512,1408]{1,0:T(8,128)(2,1)S(1)}, u32[]{:S(2)}) copy-start(bf16[512,1408]{1,0:T(8,128)(2,1)S(1)} %add_convert_fusion) | copy-start | bytes 4325380
  114.8 22.1 %collective-permute-start.10 = (bf16[512,512]{1,0:T(8,128)(2,1)S(1)}, bf16[512,512]{1,0:T(8,128)(2,1)S(1)}, u32[]{:S(2)}, u32[]{:S(2)}) collective-permute-start(bf16[512,512]{1,0:T(8,128)(2,1)S(1)} %copy-done.23), channel_id=1, source_target_pairs={{0,2},{2,0},{4,6},{6,4},{8,10},{10,8},{12,14},{14,12},{16,18},{18,... | collective-permute-start | bytes 1572872 | tf_op jit(solution)/shard_map/ppermute | solution.py:353
  115.8 1.9 copy-start.22
  115.8 3.0 %copy-start.13 = (bf16[512,1408]{1,0:T(8,128)(2,1)S(1)}, bf16[512,1408]{1,0:T(8,128)(2,1)}, u32[]{:S(2)}) copy-start(bf16[512,1408]{1,0:T(8,128)(2,1)} %get-tuple-element.93) | copy-start | bytes 4325380
  117.7 23.2 %collective-permute-start.6 = (bf16[512,512]{1,0:T(8,128)(2,1)S(1)}, bf16[512,512]{1,0:T(8,128)(2,1)S(1)}, u32[]{:S(2)}, u32[]{:S(2)}) collective-permute-start(bf16[512,512]{1,0:T(8,128)(2,1)S(1)} %copy-done.22), channel_id=1, source_target_pairs={{0,2},{2,0},{4,6},{6,4},{8,10},{10,8},{12,14},{14,12},{16,18},{18,... | collective-permute-start | bytes 1572872 | tf_op jit(solution)/shard_map/ppermute | solution.py:353
  121.4 1.9 copy-start.21
  121.4 1.9 copy-start.18
  122.4 5.0 %copy-start.19 = (bf16[512,512]{1,0:T(8,128)(2,1)S(1)}, bf16[512,512]{1,0:T(8,128)(2,1)}, u32[]{:S(2)}) copy-start(bf16[512,512]{1,0:T(8,128)(2,1)} %get-tuple-element.87) | copy-start | bytes 1572868
  123.3 20.5 %collective-permute-start.5 = (bf16[256,1024]{1,0:T(8,128)(2,1)S(1)}, bf16[256,1024]{1,0:T(8,128)(2,1)}, u32[]{:S(2)}, u32[]{:S(2)}) collective-permute-start(bf16[256,1024]{1,0:T(8,128)(2,1)S(1)} %copy-done.21), channel_id=1, source_target_pairs={{0,1},{1,0},{2,3},{3,2},{4,5},{5,4},{6,7},{7,6},{8,9},{9,8},{10,11... | collective-permute-start | bytes 1572872 | tf_op jit(solution)/shard_map/ppermute | solution.py:399
  123.5 13.4 %copy-start.8 = (bf16[512,512]{1,0:T(8,128)(2,1)}, bf16[512,512]{1,0:T(8,128)(2,1)S(1)}, u32[]{:S(2)}) copy-start(bf16[512,512]{1,0:T(8,128)(2,1)S(1)} %add_convert_fusion.6) | copy-start | bytes 1572868
  123.5 13.2 %copy-start.17 = (bf16[512,512]{1,0:T(8,128)(2,1)S(1)}, bf16[512,512]{1,0:T(8,128)(2,1)}, u32[]{:S(2)}) copy-start(bf16[512,512]{1,0:T(8,128)(2,1)} %get-tuple-element.85) | copy-start | bytes 1572868
  126.8 106.8 %collective-permute-start.36 = (bf16[256,1408]{1,0:T(8,128)(2,1)}, bf16[256,1408]{1,0:T(8,128)(2,1)}, u32[]{:S(2)}, u32[]{:S(2)}) collective-permute-start(bf16[256,1408]{1,0:T(8,128)(2,1)} %slice.312), channel_id=1, source_target_pairs={{0,2},{2,0},{4,6},{6,4},{8,10},{10,8},{12,14},{14,12},{16,18},{18,... | collective-permute-start | bytes 2162696 | tf_op jit(solution)/shard_map/ppermute | solution.py:353
  127.5 11.1 %copy-start.9 = (bf16[512,512]{1,0:T(8,128)(2,1)}, bf16[512,512]{1,0:T(8,128)(2,1)S(1)}, u32[]{:S(2)}) copy-start(bf16[512,512]{1,0:T(8,128)(2,1)S(1)} %add_convert_fusion.7) | copy-start | bytes 1572868
  127.5 10.9 %copy-start.16 = (bf16[512,512]{1,0:T(8,128)(2,1)S(1)}, bf16[512,512]{1,0:T(8,128)(2,1)}, u32[]{:S(2)}) copy-start(bf16[512,512]{1,0:T(8,128)(2,1)} %get-tuple-element.83) | copy-start | bytes 1572868
  136.2 99.2 %collective-permute-start.32 = (bf16[256,1408]{1,0:T(8,128)(2,1)}, bf16[256,1408]{1,0:T(8,128)(2,1)}, u32[]{:S(2)}, u32[]{:S(2)}) collective-permute-start(bf16[256,1408]{1,0:T(8,128)(2,1)} %slice.306), channel_id=1, source_target_pairs={{0,2},{2,0},{4,6},{6,4},{8,10},{10,8},{12,14},{14,12},{16,18},{18,... | collective-permute-start | bytes 2162696 | tf_op jit(solution)/shard_map/ppermute | solution.py:353
  136.7 4.8 %copy-start.15 = (bf16[512,512]{1,0:T(8,128)(2,1)S(1)}, bf16[512,512]{1,0:T(8,128)(2,1)}, u32[]{:S(2)}) copy-start(bf16[512,512]{1,0:T(8,128)(2,1)} %get-tuple-element.81) | copy-start | bytes 1572868
  136.9 4.8 %copy-start.10 = (bf16[512,512]{1,0:T(8,128)(2,1)}, bf16[512,512]{1,0:T(8,128)(2,1)S(1)}, u32[]{:S(2)}) copy-start(bf16[512,512]{1,0:T(8,128)(2,1)S(1)} %add_convert_fusion.8) | copy-start | bytes 1572868
  136.9 40.7 %collective-permute-start.23 = (bf16[256,512]{1,0:T(8,128)(2,1)}, bf16[256,512]{1,0:T(8,128)(2,1)}, u32[]{:S(2)}, u32[]{:S(2)}) collective-permute-start(bf16[256,512]{1,0:T(8,128)(2,1)} %slice.289), channel_id=1, source_target_pairs={{0,2},{2,0},{4,6},{6,4},{8,10},{10,8},{12,14},{14,12},{16,18},{18,... | collective-permute-start | bytes 786440 | tf_op jit(solution)/shard_map/ppermute | solution.py:353
  140.9 42.2 %collective-permute-start.19 = (bf16[256,512]{1,0:T(8,128)(2,1)}, bf16[256,512]{1,0:T(8,128)(2,1)}, u32[]{:S(2)}, u32[]{:S(2)}) collective-permute-start(bf16[256,512]{1,0:T(8,128)(2,1)} %slice.283), channel_id=1, source_target_pairs={{0,2},{2,0},{4,6},{6,4},{8,10},{10,8},{12,14},{14,12},{16,18},{18,... | collective-permute-start | bytes 786440 | tf_op jit(solution)/shard_map/ppermute | solution.py:353
  143.8 95.3 %collective-permute-start.28 = (bf16[256,1408]{1,0:T(8,128)(2,1)}, bf16[256,1408]{1,0:T(8,128)(2,1)}, u32[]{:S(2)}, u32[]{:S(2)}) collective-permute-start(bf16[256,1408]{1,0:T(8,128)(2,1)} %slice.300), channel_id=1, source_target_pairs={{0,4},{2,6},{4,0},{6,2},{8,12},{10,14},{12,8},{14,10},{16,20},{18,... | collective-permute-start | bytes 2162696 | tf_op jit(solution)/shard_map/ppermute | solution.py:353
  147.8 38.4 %copy-start.20 = (bf16[256,512]{1,0:T(8,128)(2,1)S(1)}, bf16[256,512]{1,0:T(8,128)(2,1)}, u32[]{:S(2)}) copy-start(bf16[256,512]{1,0:T(8,128)(2,1)} %slice.265) | copy-start | bytes 786436
  147.8 39.0 %copy-start.11 = (bf16[512,512]{1,0:T(8,128)(2,1)S(1)}, bf16[512,512]{1,0:T(8,128)(2,1)}, u32[]{:S(2)}) copy-start(bf16[512,512]{1,0:T(8,128)(2,1)} %copy-done.10) | copy-start | bytes 1572868
  177.5 8.7 %collective-permute-start.15 = (bf16[256,512]{1,0:T(8,128)(2,1)}, bf16[256,512]{1,0:T(8,128)(2,1)S(1)}, u32[]{:S(2)}, u32[]{:S(2)}) collective-permute-start(bf16[256,512]{1,0:T(8,128)(2,1)} %slice.277), channel_id=1, source_target_pairs={{0,2},{2,0},{4,6},{6,4},{8,10},{10,8},{12,14},{14,12},{16,18},{18,... | collective-permute-start | bytes 786440 | tf_op jit(solution)/shard_map/ppermute | solution.py:353
  183.1 9.3 %collective-permute-start.11 = (bf16[256,512]{1,0:T(8,128)(2,1)}, bf16[256,512]{1,0:T(8,128)(2,1)S(1)}, u32[]{:S(2)}, u32[]{:S(2)}) collective-permute-start(bf16[256,512]{1,0:T(8,128)(2,1)} %slice.271), channel_id=1, source_target_pairs={{0,4},{2,6},{4,0},{6,2},{8,12},{10,14},{12,8},{14,10},{16,20},{18,... | collective-permute-start | bytes 786440 | tf_op jit(solution)/shard_map/ppermute | solution.py:353
  186.2 10.1 %collective-permute-start.7 = (bf16[256,512]{1,0:T(8,128)(2,1)S(1)}, bf16[256,512]{1,0:T(8,128)(2,1)S(1)}, u32[]{:S(2)}, u32[]{:S(2)}) collective-permute-start(bf16[256,512]{1,0:T(8,128)(2,1)S(1)} %copy-done.20), channel_id=1, source_target_pairs={{0,4},{2,6},{4,0},{6,2},{8,12},{10,14},{12,8},{14,10},{16,20},{18,... | collective-permute-start | bytes 786440 | tf_op jit(solution)/shard_map/ppermute | solution.py:353
  192.5 5.5 %collective-permute-start.24 = (bf16[128,512]{1,0:T(8,128)(2,1)S(1)}, bf16[128,512]{1,0:T(8,128)(2,1)S(1)}, u32[]{:S(2)}, u32[]{:S(2)}) collective-permute-start(bf16[128,512]{1,0:T(8,128)(2,1)S(1)} %slice.291), channel_id=1, source_target_pairs={{0,4},{2,6},{4,0},{6,2},{8,12},{10,14},{12,8},{14,10},{16,20},{18,... | collective-permute-start | bytes 393224 | tf_op jit(solution)/shard_map/ppermute | solution.py:353
  196.3 9.6 %collective-permute-start.20 = (bf16[128,512]{1,0:T(8,128)(2,1)S(1)}, bf16[128,512]{1,0:T(8,128)(2,1)S(1)}, u32[]{:S(2)}, u32[]{:S(2)}) collective-permute-start(bf16[128,512]{1,0:T(8,128)(2,1)S(1)} %slice.285), channel_id=1, source_target_pairs={{0,8},{2,10},{4,12},{6,14},{8,0},{10,2},{12,4},{14,6},{16,24},{18,... | collective-permute-start | bytes 393224 | tf_op jit(solution)/shard_map/ppermute | solution.py:353
  198.0 6.4 %collective-permute-start.8 = (bf16[128,512]{1,0:T(8,128)(2,1)S(1)}, bf16[128,512]{1,0:T(8,128)(2,1)S(1)}, u32[]{:S(2)}, u32[]{:S(2)}) collective-permute-start(bf16[128,512]{1,0:T(8,128)(2,1)S(1)} %slice.267), channel_id=1, source_target_pairs={{0,8},{2,10},{4,12},{6,14},{8,0},{10,2},{12,4},{14,6},{16,24},{18,... | collective-permute-start | bytes 393224 | tf_op jit(solution)/shard_map/ppermute | solution.py:353
  204.4 5.2 %collective-permute-start.16 = (bf16[128,512]{1,0:T(8,128)(2,1)S(1)}, bf16[128,512]{1,0:T(8,128)(2,1)S(1)}, u32[]{:S(2)}, u32[]{:S(2)}) collective-permute-start(bf16[128,512]{1,0:T(8,128)(2,1)S(1)} %slice.279), channel_id=1, source_target_pairs={{0,8},{2,10},{4,12},{6,14},{8,0},{10,2},{12,4},{14,6},{16,24},{18,... | collective-permute-start | bytes 393224 | tf_op jit(solution)/shard_map/ppermute | solution.py:353
  205.9 27.7 %copy-start.2 = (bf16[512,1408]{1,0:T(8,128)(2,1)S(1)}, bf16[512,1408]{1,0:T(8,128)(2,1)}, u32[]{:S(2)}) copy-start(bf16[512,1408]{1,0:T(8,128)(2,1)} %copy-done.1) | copy-start | bytes 4325380
  205.9 6.6 %collective-permute-start.12 = (bf16[128,512]{1,0:T(8,128)(2,1)S(1)}, bf16[128,512]{1,0:T(8,128)(2,1)S(1)}, u32[]{:S(2)}, u32[]{:S(2)}) collective-permute-start(bf16[128,512]{1,0:T(8,128)(2,1)S(1)} %slice.273), channel_id=1, source_target_pairs={{0,8},{2,10},{4,12},{6,14},{8,0},{10,2},{12,4},{14,6},{16,24},{18,... | collective-permute-start | bytes 393224 | tf_op jit(solution)/shard_map/ppermute | solution.py:353
  209.6 23.9 %collective-permute-start.25 = (bf16[64,512]{1,0:T(8,128)(2,1)S(1)}, bf16[64,512]{1,0:T(8,128)(2,1)S(1)}, u32[]{:S(2)}, u32[]{:S(2)}) collective-permute-start(bf16[64,512]{1,0:T(8,128)(2,1)S(1)} %slice.293), channel_id=1, source_target_pairs={{0,16},{2,18},{4,20},{6,22},{8,24},{10,26},{12,28},{14,30},{16,0},... | collective-permute-start | bytes 196616 | tf_op jit(solution)/shard_map/ppermute | solution.py:353
  212.5 5.2 %collective-permute-start.9 = (bf16[64,512]{1,0:T(8,128)(2,1)S(1)}, bf16[64,512]{1,0:T(8,128)(2,1)S(1)}, u32[]{:S(2)}, u32[]{:S(2)}) collective-permute-start(bf16[64,512]{1,0:T(8,128)(2,1)S(1)} %slice.269), channel_id=1, source_target_pairs={{0,16},{2,18},{4,20},{6,22},{8,24},{10,26},{12,28},{14,30},{16,0},... | collective-permute-start | bytes 196616 | tf_op jit(solution)/shard_map/ppermute | solution.py:353
  217.7 5.2 %collective-permute-start.13 = (bf16[64,512]{1,0:T(8,128)(2,1)S(1)}, bf16[64,512]{1,0:T(8,128)(2,1)S(1)}, u32[]{:S(2)}, u32[]{:S(2)}) collective-permute-start(bf16[64,512]{1,0:T(8,128)(2,1)S(1)} %slice.275), channel_id=1, source_target_pairs={{0,16},{2,18},{4,20},{6,22},{8,24},{10,26},{12,28},{14,30},{16,0},... | collective-permute-start | bytes 196616 | tf_op jit(solution)/shard_map/ppermute | solution.py:353
  222.9 5.4 %collective-permute-start.17 = (bf16[64,512]{1,0:T(8,128)(2,1)S(1)}, bf16[64,512]{1,0:T(8,128)(2,1)S(1)}, u32[]{:S(2)}, u32[]{:S(2)}) collective-permute-start(bf16[64,512]{1,0:T(8,128)(2,1)S(1)} %slice.281), channel_id=1, source_target_pairs={{0,16},{2,18},{4,20},{6,22},{8,24},{10,26},{12,28},{14,30},{16,0},... | collective-permute-start | bytes 196616 | tf_op jit(solution)/shard_map/ppermute | solution.py:353
  228.3 5.2 %collective-permute-start.21 = (bf16[64,512]{1,0:T(8,128)(2,1)S(1)}, bf16[64,512]{1,0:T(8,128)(2,1)S(1)}, u32[]{:S(2)}, u32[]{:S(2)}) collective-permute-start(bf16[64,512]{1,0:T(8,128)(2,1)S(1)} %slice.287), channel_id=1, source_target_pairs={{0,16},{2,18},{4,20},{6,22},{8,24},{10,26},{12,28},{14,30},{16,0},... | collective-permute-start | bytes 196616 | tf_op jit(solution)/shard_map/ppermute | solution.py:353
  233.6 30.0 %collective-permute-start.26 = (f32[5,64,512]{2,1,0:T(8,128)S(1)}, f32[5,64,512]{2,1,0:T(8,128)S(1)}, u32[]{:S(2)}, u32[]{:S(2)}) collective-permute-start(f32[5,64,512]{2,1,0:T(8,128)S(1)} %bitcast_dynamic-update-slice_fusion), channel_id=1, source_target_pairs={{0,1},{1,0},{2,3},{3,2},{4,5},{5,4},{6,7},{7,6},{8,9},{9,8},{10,11... | collective-permute-start | bytes 1966088 | tf_op jit(solution)/shard_map/ppermute | solution.py:399
  235.0 10.9 %collective-permute-start.37 = (bf16[128,1408]{1,0:T(8,128)(2,1)S(1)}, bf16[128,1408]{1,0:T(8,128)(2,1)S(1)}, u32[]{:S(2)}, u32[]{:S(2)}) collective-permute-start(bf16[128,1408]{1,0:T(8,128)(2,1)S(1)} %slice.314), channel_id=1, source_target_pairs={{0,4},{2,6},{4,0},{6,2},{8,12},{10,14},{12,8},{14,10},{16,20},{18,... | collective-permute-start | bytes 1081352 | tf_op jit(solution)/shard_map/ppermute | solution.py:353
  236.7 11.6 %collective-permute-start.33 = (bf16[128,1408]{1,0:T(8,128)(2,1)S(1)}, bf16[128,1408]{1,0:T(8,128)(2,1)S(1)}, u32[]{:S(2)}, u32[]{:S(2)}) collective-permute-start(bf16[128,1408]{1,0:T(8,128)(2,1)S(1)} %slice.308), channel_id=1, source_target_pairs={{0,8},{2,10},{4,12},{6,14},{8,0},{10,2},{12,4},{14,6},{16,24},{18,... | collective-permute-start | bytes 1081352 | tf_op jit(solution)/shard_map/ppermute | solution.py:353
  240.4 22.9 %collective-permute-start.29 = (bf16[128,1408]{1,0:T(8,128)(2,1)S(1)}, bf16[128,1408]{1,0:T(8,128)(2,1)S(1)}, u32[]{:S(2)}, u32[]{:S(2)}) collective-permute-start(bf16[128,1408]{1,0:T(8,128)(2,1)S(1)} %slice.302), channel_id=1, source_target_pairs={{0,8},{2,10},{4,12},{6,14},{8,0},{10,2},{12,4},{14,6},{16,24},{18,... | collective-permute-start | bytes 1081352 | tf_op jit(solution)/shard_map/ppermute | solution.py:353
  246.0 18.8 %collective-permute-start.38 = (bf16[64,1408]{1,0:T(8,128)(2,1)S(1)}, bf16[64,1408]{1,0:T(8,128)(2,1)S(1)}, u32[]{:S(2)}, u32[]{:S(2)}) collective-permute-start(bf16[64,1408]{1,0:T(8,128)(2,1)S(1)} %slice.316), channel_id=1, source_target_pairs={{0,16},{2,18},{4,20},{6,22},{8,24},{10,26},{12,28},{14,30},{16,0},... | collective-permute-start | bytes 540680 | tf_op jit(solution)/shard_map/ppermute | solution.py:353
  248.4 17.2 %collective-permute-start.34 = (bf16[64,1408]{1,0:T(8,128)(2,1)S(1)}, bf16[64,1408]{1,0:T(8,128)(2,1)S(1)}, u32[]{:S(2)}, u32[]{:S(2)}) collective-permute-start(bf16[64,1408]{1,0:T(8,128)(2,1)S(1)} %slice.310), channel_id=1, source_target_pairs={{0,16},{2,18},{4,20},{6,22},{8,24},{10,26},{12,28},{14,30},{16,0},... | collective-permute-start | bytes 540680 | tf_op jit(solution)/shard_map/ppermute | solution.py:353
  263.4 10.0 %collective-permute-start.30 = (bf16[64,1408]{1,0:T(8,128)(2,1)S(1)}, bf16[64,1408]{1,0:T(8,128)(2,1)S(1)}, u32[]{:S(2)}, u32[]{:S(2)}) collective-permute-start(bf16[64,1408]{1,0:T(8,128)(2,1)S(1)} %slice.304), channel_id=1, source_target_pairs={{0,16},{2,18},{4,20},{6,22},{8,24},{10,26},{12,28},{14,30},{16,0},... | collective-permute-start | bytes 540680 | tf_op jit(solution)/shard_map/ppermute | solution.py:353
